TPU v7x, 32 devices: a whole 2x2x4 slice. The times are simulated.
32 devices in a mesh: block: 8 (over y, x, core), dp: 4 (over z).
Axes of the slice: x: 2, y: 2, z: 4, core: 2. Of those that a mesh axis runs over, the one named last changes fastest.
Arguments:
- tokens: bfloat16 [2048, 12288], P('dp', 'block'), may hold values from -6 to 6
- cotangent: bfloat16 [2048, 12288], P('dp', 'block'), may hold values from -12 to 12
- right_one: bfloat16 [96, 128, 384], P('block'), may hold values from -0.5 to 0.5
- left_one: bfloat16 [96, 384, 512], P('block'), may hold values from -0.3125 to 0.3125
- right_two: bfloat16 [96, 512, 384], P('block'), may hold values from -0.25 to 0.25
- left_two: bfloat16 [96, 384, 128], P('block'), may hold values from -0.3125 to 0.3125
- grad_prev: float32 [96, 491520], P('block', 'dp'), may hold values from -12 to 12
- moment_one: float32 [96, 491520], P('block', 'dp'), may hold values from -2 to 2
- moment_two: float32 [96, 491520], P('block', 'dp'), may hold values from 0.05 to 4
Outputs:
- grad_tokens: bfloat16 [2048, 12288], P('dp', 'block')
- grad_right_one: float32 [96, 128, 384], P('block', 'dp')
- grad_left_one: float32 [96, 384, 512], P('block', 'dp')
- grad_right_two: float32 [96, 512, 384], P('block', 'dp')
- grad_left_two: float32 [96, 384, 128], P('block', 'dp')
- new_moment_one: float32 [96, 491520], P('block', 'dp')
- new_moment_two: float32 [96, 491520], P('block', 'dp')
- adam_update: float32 [96, 491520], P('block', 'dp')
All inputs are finite; a program needn't handle non-finite values.
Results may differ from a plain program's by a relative error of at most 0.013.
Values may be sent and summed in bfloat16 or wider, within the bound.
No kernel may reach another device: no remote copies, remote signals or barrier semaphores. Data moves between devices by JAX's collectives and lax.ppermute only.
A program may use at most 192 MiB of HBM per device.

v0:
```python
import jax
import jax.numpy as jnp
from jax import lax
from jax.sharding import PartitionSpec as P

BLOCKS = 96
SPLIT = 4
BLOCK_IN = 128
BLOCK_HID = 512
MIDDLE = 384


def gelu_tanh(values):
    return jax.nn.gelu(values, approximate=True)


def on_device(
    tokens, cotangent, right_one, left_one, right_two, left_two, grad_prev, moment_one, moment_two
):
    f32 = jnp.float32
    bf16 = jnp.bfloat16
    row_count = tokens.shape[0]
    blocks_here = right_one.shape[0]
    loss_scale = float(lax.axis_size("dp") * row_count) ** (-0.5)
    new_moment_one = 0.9 * moment_one + 0.1 * grad_prev
    new_moment_two = 0.95 * moment_two + 0.05 * grad_prev * grad_prev
    first_hat = new_moment_one / (1.0 - 0.9**10)
    second_hat = new_moment_two / (1.0 - 0.95**10)
    adam_update = first_hat / (jnp.sqrt(second_hat) + 1e-08)
    token_blocks = tokens.reshape(row_count, blocks_here, BLOCK_IN)
    first_mid = jnp.einsum(
        "tbk,bkj->bjt", token_blocks, right_one, preferred_element_type=f32
    ).astype(bf16)
    first_in = lax.all_to_all(
        first_mid.reshape(blocks_here, BLOCKS, SPLIT, row_count),
        "block",
        split_axis=1,
        concat_axis=0,
        tiled=True,
    )
    left_first = left_one.reshape(blocks_here, BLOCKS, SPLIT, BLOCK_HID)
    hidden_pre = jnp.einsum("bcqt,cbqf->cft", first_in, left_first, preferred_element_type=f32)
    hidden = gelu_tanh(hidden_pre).astype(bf16)
    second_mid = jnp.einsum("cft,cfj->cjt", hidden, right_two, preferred_element_type=f32).astype(
        bf16
    )
    second_in = lax.all_to_all(
        second_mid.reshape(blocks_here, BLOCKS, SPLIT, row_count),
        "block",
        split_axis=1,
        concat_axis=0,
        tiled=True,
    )
    left_second = left_two.reshape(blocks_here, BLOCKS, SPLIT, BLOCK_IN)
    grad_blocks = cotangent.reshape(row_count, blocks_here, BLOCK_IN)
    grad_second_out = jnp.einsum(
        "tdk,dcqk->cdqt", grad_blocks, left_second, preferred_element_type=f32
    ).astype(bf16)
    grad_left_two = (
        jnp.einsum("cdqt,tdk->dcqk", second_in, grad_blocks, preferred_element_type=f32)
        * loss_scale
    )
    grad_left_two = grad_left_two.reshape(blocks_here, MIDDLE, BLOCK_IN)
    grad_second = lax.all_to_all(grad_second_out, "block", split_axis=0, concat_axis=1, tiled=True)
    grad_second = grad_second.reshape(blocks_here, MIDDLE, row_count)
    grad_right_two = (
        jnp.einsum("cft,cjt->cfj", hidden, grad_second, preferred_element_type=f32) * loss_scale
    )
    grad_hidden = jnp.einsum("cjt,cfj->cft", grad_second, right_two, preferred_element_type=f32)
    unused_value, back_gelu = jax.vjp(gelu_tanh, hidden_pre)
    grad_pre = back_gelu(grad_hidden)[0].astype(bf16)
    grad_left_one = (
        jnp.einsum("bcqt,cft->cbqf", first_in, grad_pre, preferred_element_type=f32) * loss_scale
    )
    grad_left_one = grad_left_one.reshape(blocks_here, MIDDLE, BLOCK_HID)
    grad_first_out = jnp.einsum(
        "cft,cbqf->bcqt", grad_pre, left_first, preferred_element_type=f32
    ).astype(bf16)
    grad_first = lax.all_to_all(grad_first_out, "block", split_axis=0, concat_axis=1, tiled=True)
    grad_first = grad_first.reshape(blocks_here, MIDDLE, row_count)
    grad_right_one = (
        jnp.einsum("tbk,bjt->bkj", token_blocks, grad_first, preferred_element_type=f32)
        * loss_scale
    )
    grad_inputs = jnp.einsum(
        "bjt,bkj->tbk", grad_first, right_one, preferred_element_type=f32
    ).astype(bf16)
    grad_tokens = grad_inputs.reshape(row_count, blocks_here * BLOCK_IN)
    sum_right_one, sum_left_one, sum_right_two, sum_left_two = (
        lax.psum_scatter(
            grad_right_one.astype(jnp.bfloat16), "dp", scatter_dimension=1, tiled=True
        ).astype(jnp.float32),
        lax.psum_scatter(
            grad_left_one.astype(jnp.bfloat16), "dp", scatter_dimension=1, tiled=True
        ).astype(jnp.float32),
        lax.psum_scatter(
            grad_right_two.astype(jnp.bfloat16), "dp", scatter_dimension=1, tiled=True
        ).astype(jnp.float32),
        lax.psum_scatter(
            grad_left_two.astype(jnp.bfloat16), "dp", scatter_dimension=1, tiled=True
        ).astype(jnp.float32),
    )
    return (
        grad_tokens,
        sum_right_one,
        sum_left_one,
        sum_right_two,
        sum_left_two,
        new_moment_one,
        new_moment_two,
        adam_update,
    )


def solution(mesh):
    in_specs = (
        P("dp", "block"),
        P("dp", "block"),
        P("block", None, None),
        P("block", None, None),
        P("block", None, None),
        P("block", None, None),
        P("block", "dp"),
        P("block", "dp"),
        P("block", "dp"),
    )
    out_specs = (
        P("dp", "block"),
        P("block", "dp", None),
        P("block", "dp", None),
        P("block", "dp", None),
        P("block", "dp", None),
        P("block", "dp"),
        P("block", "dp"),
        P("block", "dp"),
    )
    return jax.shard_map(
        on_device, mesh=mesh, in_specs=in_specs, out_specs=out_specs, check_vma=False
    )
```

profile of v0, /device:TPU:0, one launch (start us, length us, event | category | flops | bytes accessed | tf_op | source)
XLA Modules:
  0.0 509.3 jit_solution(12045664359937483489)
XLA Ops:
  12.6 7.7 %reshape.53 = bf16[12,96,4,512]{3,2,1,0:T(4,128)(2,1)} reshape(bf16[12,384,512]{2,1,0:T(8,128)(2,1)} %convolution_convert_fusion) | data formatting | bytes 9437184 | tf_op jit(solution)/shard_map/reshape | solution.py:35
  20.3 7.2 %copy.102 = bf16[12,96,4,512]{3,2,0,1:T(4,128)(2,1)} copy(bf16[12,96,4,512]{3,2,1,0:T(4,128)(2,1)} %reshape.53) | data formatting | bytes 9437184 | tf_op jit(solution)/shard_map/reshape | solution.py:35
  43.5 44.1 %all-to-all-done.1 = bf16[12,96,4,512]{3,2,0,1:T(4,128)(2,1)} async-done(((bf16[12,96,4,512]{3,2,0,1:T(4,128)(2,1)}), bf16[12,96,4,512]{3,2,0,1:T(4,128)(2,1)}, u32[]{:S(2)}, u32[]{:S(2)}) %all-to-all-start.1) | async-done | bytes 4718624 | tf_op jit(solution)/shard_map/all_to_all | solution.py:34
  92.4 7.7 %reshape.54 = bf16[12,96,4,512]{3,2,1,0:T(4,128)(2,1)} reshape(bf16[12,384,512]{2,1,0:T(8,128)(2,1)} %param.12) | data formatting | bytes 9437184 | tf_op jit(solution)/shard_map/reshape | solution.py:41
  100.1 7.3 %copy.104 = bf16[8,12,12,4,512]{4,3,2,1,0:T(4,128)(2,1)} copy(bf16[8,12,12,4,512]{4,3,1,2,0:T(4,128)(2,1)} %bitcast.10) | data formatting | bytes 9437184 | tf_op jit(solution)/shard_map/all_to_all | solution.py:34
  107.4 9.2 %fusion.19 = f32[12,512,512,1]{2,1,3,0:T(8,128)S(1)} fusion(bf16[12,96,4,512]{3,2,1,0:T(4,128)(2,1)} %reshape.54, bf16[96,12,4,512]{3,2,1,0:T(4,128)(2,1)} %bitcast.89), kind=kOutput, calls=%fused_computation.32 | convolution fusion | flops 2415919104 | bytes 22020096 | tf_op jit(solution)/shard_map/bcqt,cbqf->cft/dot_general | solution.py:42
  121.1 10.0 %convert_bitcast_fusion = bf16[12,384,512]{2,1,0:T(8,128)(2,1)} fusion(bf16[12,512,384]{2,1,0:T(8,128)(2,1)} %param.13, f32[12,512,512,1]{2,1,3,0:T(8,128)S(1)} %fusion.19), kind=kOutput, calls=%fused_computation.28 | convolution fusion | flops 2446589952 | bytes 22020096 | tf_op jit(solution)/shard_map/cft,cfj->cjt/dot_general | solution.py:44
  131.1 7.7 %reshape.57 = bf16[12,96,4,512]{3,2,1,0:T(4,128)(2,1)} reshape(bf16[12,384,512]{2,1,0:T(8,128)(2,1)} %convert_bitcast_fusion) | data formatting | bytes 9437184 | tf_op jit(solution)/shard_map/reshape | solution.py:48
  138.8 7.2 %copy.119 = bf16[12,96,4,512]{3,2,0,1:T(4,128)(2,1)} copy(bf16[12,96,4,512]{3,2,1,0:T(4,128)(2,1)} %reshape.57) | data formatting | bytes 9437184 | tf_op jit(solution)/shard_map/reshape | solution.py:48
  152.2 7.4 %copy.97 = bf16[12,8,12,4,512]{4,3,2,1,0:T(4,128)(2,1)} copy(bf16[12,8,12,4,512]{4,3,2,0,1:T(4,128)(2,1)} %bitcast.5) | data formatting | bytes 9437184 | tf_op jit(solution)/shard_map/all_to_all | solution.py:64
  159.6 7.7 %reshape.51 = bf16[12,384,512]{2,1,0:T(8,128)(2,1)} reshape(bf16[12,8,12,4,512]{4,3,2,1,0:T(4,128)(2,1)} %copy.97) | data formatting | bytes 9437184 | tf_op jit(solution)/shard_map/reshape | solution.py:65
  167.3 16.6 %fusion.6 = bf16[12,512,512]{1,2,0:T(8,128)(2,1)} fusion(f32[12,512,512,1]{2,1,3,0:T(8,128)} %copy-done.1, bf16[12,384,512]{2,1,0:T(8,128)(2,1)} %reshape.51, bf16[12,512,384]{2,1,0:T(8,128)(2,1)} %param.13), kind=kOutput, calls=%fused_computation.8 | convolution fusion | flops 2478833664 | bytes 28311552 | tf_op jit(solution)/shard_map/cjt,cfj->cft/dot_general | solution.py:69
  184.0 9.0 %convert_bitcast_fusion.1 = bf16[96,12,4,512]{3,0,2,1:T(8,128)(2,1)} fusion(bf16[12,96,4,512]{3,2,1,0:T(4,128)(2,1)} %reshape.54, bf16[12,512,512]{1,2,0:T(8,128)(2,1)} %fusion.6), kind=kOutput, calls=%fused_computation.29 | convolution fusion | flops 2418278400 | bytes 15728640 | tf_op jit(solution)/shard_map/cft,cbqf->bcqt/dot_general | solution.py:76
  193.0 8.2 %copy.109 = bf16[96,12,4,512]{3,2,1,0:T(4,128)(2,1)} copy(bf16[96,12,4,512]{3,0,2,1:T(8,128)(2,1)} %convert_bitcast_fusion.1) | data formatting | bytes 9437184 | tf_op jit(solution)/shard_map/convert_element_type | solution.py:78
  224.0 42.3 %all-to-all-done.2 = bf16[96,12,4,512]{3,2,1,0:T(4,128)(2,1)} async-done(((bf16[96,12,4,512]{3,2,1,0:T(4,128)(2,1)}), bf16[96,12,4,512]{3,2,1,0:T(4,128)(2,1)}, u32[]{:S(2)}, u32[]{:S(2)}) %all-to-all-start.2) | async-done | bytes 4718624 | tf_op jit(solution)/shard_map/all_to_all | solution.py:79
  266.3 7.4 %copy.110 = bf16[12,8,12,4,512]{4,3,2,1,0:T(4,128)(2,1)} copy(bf16[12,8,12,4,512]{4,3,2,0,1:T(4,128)(2,1)} %bitcast.19) | data formatting | bytes 9437184 | tf_op jit(solution)/shard_map/all_to_all | solution.py:79
  273.7 7.8 %reshape.55 = bf16[12,384,512]{2,1,0:T(8,128)(2,1)} reshape(bf16[12,8,12,4,512]{4,3,2,1,0:T(4,128)(2,1)} %copy.110) | data formatting | bytes 9437184 | tf_op jit(solution)/shard_map/reshape | solution.py:80
  289.5 12.1 %multiply_convert_fusion = bf16[12,512,384]{2,1,0:T(8,128)(2,1)} fusion(bf16[12,384,512]{2,1,0:T(8,128)(2,1)} %reshape.51, f32[12,512,512,1]{2,1,3,0:T(8,128)} %copy-done.1), kind=kOutput, calls=%fused_computation.17 | convolution fusion | flops 2448949248 | bytes 22020096 | tf_op jit(solution)/shard_map/cft,cjt->cfj/dot_general | solution.py:67
  301.7 9.4 %multiply_convert_fusion.1 = bf16[12,96,4,512]{3,1,2,0:T(8,128)(2,1)S(1)} fusion(bf16[12,512,512]{1,2,0:T(8,128)(2,1)} %fusion.6, bf16[96,12,4,512]{3,2,1,0:T(4,128)(2,1)} %bitcast.90), kind=kOutput, calls=%fused_computation.18 | convolution fusion | flops 2420637696 | bytes 15728640 | tf_op jit(solution)/shard_map/bcqt,cft->cbqf/dot_general | solution.py:73
  311.1 5.8 %copy.115 = bf16[12,96,4,512]{3,2,1,0:T(4,128)(2,1)} copy(bf16[12,96,4,512]{3,1,2,0:T(8,128)(2,1)S(1)} %multiply_convert_fusion.1) | data formatting | bytes 9437184 | tf_op jit(solution)/shard_map/convert_element_type | solution.py:94
  316.9 8.0 %convert_element_type.78 = bf16[12,384,512]{2,1,0:T(8,128)(2,1)} reshape(bf16[12,96,4,512]{3,2,1,0:T(4,128)(2,1)} %copy.115) | data formatting | bytes 9437184 | tf_op jit(solution)/shard_map/convert_element_type | solution.py:94
  324.9 18.0 %add_divide_fusion = (f32[12,122880]{1,0:T(8,128)}, f32[12,122880]{1,0:T(8,128)}, f32[12,122880]{1,0:T(8,128)}) fusion(f32[12,122880]{1,0:T(8,128)} %param.15, f32[12,122880]{1,0:T(8,128)} %param.17, f32[12,122880]{1,0:T(8,128)} %param.16), kind=kLoop, calls=%fused_computation.20 | loop fusion | flops 16220160 | bytes 35389440 | tf_op jit(solution)/shard_map/div | solution.py:29
  349.2 62.2 %reduce-scatter.9.cloned.1.call-done = bf16[12,128,384]{2,1,0:T(8,128)(2,1)} async-done(((bf16[12,512,384]{2,1,0:T(8,128)(2,1)}), bf16[12,128,384]{2,1,0:T(8,128)(2,1)}) %reduce-scatter.9.cloned.1.call-update) | async-done | bytes 1179664 | tf_op jit(solution)/shard_map/reduce_scatter | solution.py:96
  414.3 85.1 %reduce-scatter.7.cloned.1.call-done = bf16[12,96,512]{2,1,0:T(8,128)(2,1)} async-done(((bf16[12,384,512]{2,1,0:T(8,128)(2,1)}), bf16[12,96,512]{2,1,0:T(8,128)(2,1)}) %reduce-scatter.7.cloned.1.call-update) | async-done | bytes 1179664 | tf_op jit(solution)/shard_map/reduce_scatter | solution.py:93
  (49 shorter events, 79.9 us)
Async XLA Ops:
  7.2 1.9 copy-start
  9.0 11.3 %copy-start.2 = (bf16[512,1536]{0,1:T(8,128)(2,1)}, bf16[512,1536]{0,1:T(8,128)(2,1)S(1)}, u32[]{:S(2)}) copy-start(bf16[512,1536]{0,1:T(8,128)(2,1)S(1)} %copy.99) | copy-start | bytes 4718596
  27.5 60.0 %all-to-all-start.1 = ((bf16[12,96,4,512]{3,2,0,1:T(4,128)(2,1)}), bf16[12,96,4,512]{3,2,0,1:T(4,128)(2,1)}, u32[]{:S(2)}, u32[]{:S(2)}) async-start(bf16[12,96,4,512]{3,2,0,1:T(4,128)(2,1)} %copy.102), calls=%async_computation.1 | async-start | bytes 9437184 | tf_op jit(solution)/shard_map/all_to_all | solution.py:34
  34.4 9.1 %copy-start.4 = (bf16[512,1536]{0,1:T(8,128)(2,1)}, bf16[512,1536]{0,1:T(8,128)(2,1)S(1)}, u32[]{:S(2)}) copy-start(bf16[512,1536]{0,1:T(8,128)(2,1)S(1)} %copy.93) | copy-start | bytes 4718596
  87.5 59.6 %all-to-all-start = ((bf16[96,12,4,512]{3,2,1,0:T(4,128)(2,1)}), bf16[96,12,4,512]{3,2,1,0:T(4,128)(2,1)}, u32[]{:S(2)}, u32[]{:S(2)}) async-start(bf16[96,12,4,512]{3,2,1,0:T(4,128)(2,1)} %copy.96), calls=%async_computation | async-start | bytes 9437184 | tf_op jit(solution)/shard_map/all_to_all | solution.py:64
  116.6 4.5 copy-start.1
  147.2 59.8 %all-to-all-start.3 = ((bf16[12,96,4,512]{3,2,0,1:T(4,128)(2,1)}), bf16[12,96,4,512]{3,2,0,1:T(4,128)(2,1)}, u32[]{:S(2)}, u32[]{:S(2)}) async-start(bf16[12,96,4,512]{3,2,0,1:T(4,128)(2,1)} %copy.119), calls=%async_computation.6 | async-start | bytes 9437184 | tf_op jit(solution)/shard_map/all_to_all | solution.py:47
  206.9 59.3 %all-to-all-start.2 = ((bf16[96,12,4,512]{3,2,1,0:T(4,128)(2,1)}), bf16[96,12,4,512]{3,2,1,0:T(4,128)(2,1)}, u32[]{:S(2)}, u32[]{:S(2)}) async-start(bf16[96,12,4,512]{3,2,1,0:T(4,128)(2,1)} %copy.109), calls=%async_computation.2 | async-start | bytes 9437184 | tf_op jit(solution)/shard_map/all_to_all | solution.py:79
  211.5 133.9 %reduce-scatter.11.cloned.1.call-start = ((), (), s32[]{:S(2)}) async-start(), calls=%async_computation.11 | async-start | bytes 1474560 | tf_op jit(solution)/shard_map/reduce_scatter | solution.py:99
  211.8 5.2 %copy-start.5 = (bf16[512,1536]{0,1:T(8,128)(2,1)S(1)}, bf16[512,1536]{0,1:T(8,128)(2,1)}, u32[]{:S(2)}) copy-start(bf16[512,1536]{0,1:T(8,128)(2,1)} %copy-done.4) | copy-start | bytes 4718596
  224.0 123.3 %reduce-scatter.5.cloned.1.call-start = ((), (), s32[]{:S(2)}) async-start(), calls=%async_computation.8 | async-start | bytes 1966080 | tf_op jit(solution)/shard_map/reduce_scatter | solution.py:90
  273.7 7.8 %copy-start.3 = (bf16[512,1536]{0,1:T(8,128)(2,1)S(1)}, bf16[512,1536]{0,1:T(8,128)(2,1)}, u32[]{:S(2)}) copy-start(bf16[512,1536]{0,1:T(8,128)(2,1)} %copy-done.2) | copy-start | bytes 4718596
  289.2 122.2 %reduce-scatter.9.cloned.1.call-start = ((), (), s32[]{:S(2)}) async-start(), calls=%async_computation.10 | async-start | bytes 5898240 | tf_op jit(solution)/shard_map/reduce_scatter | solution.py:96
  301.6 197.8 %reduce-scatter.7.cloned.1.call-start = ((), (), s32[]{:S(2)}) async-start(), calls=%async_computation.9 | async-start | bytes 5898240 | tf_op jit(solution)/shard_map/reduce_scatter | solution.py:93
  324.8 18.0 %slice-start = ((s8[4718592]{0:T(1024)(128)(4,1)}), s8[524288]{0:T(1024)(128)(4,1)S(1)}, s32[]{:S(2)}) async-start(s8[4718592]{0:T(1024)(128)(4,1)} %bitcast.91), calls=%async_computation.12 | async-start | bytes 1048576
  324.9 18.0 %slice-start.1 = ((s8[4718592]{0:T(1024)(128)(4,1)}), s8[4194304]{0:T(1024)(128)(4,1)S(1)}, s32[]{:S(2)}) async-start(s8[4718592]{0:T(1024)(128)(4,1)} %bitcast.91), calls=%async_computation.13 | async-start | bytes 8388608
Sparse Core Ops, SparseCore 0:
  224.1 31.5 reduce-scatter.10
  289.3 35.4 reduce-scatter.4
  327.1 84.2 reduce-scatter.8
  413.6 85.7 reduce-scatter.6
where the time goes:
time: 518 us; the launch traced here: 509 us
  waiting for transfers between devices  241 us (47%)
  local copies, waits for them, and re-layouts  124 us (24%)
  matrix products  84.2 us (16%)
  other arithmetic  25.7 us (5%)
  starting transfers between devices  20.2 us (4%)
  between operations  14.4 us (3%)
    reduce_scatter x1, waiting for transfers between devices, on_device(): lax.psum_scatter(grad_left_one.astype(jnp.bfloat16), 'dp', scatter_dimens...  85.1 us
    reduce_scatter x1, waiting for transfers between devices, on_device(): lax.psum_scatter(grad_right_two.astype(jnp.bfloat16), 'dp', scatter_dimen...  62.2 us
    all_to_all x1, waiting for transfers between devices, on_device(): lax.all_to_all(first_mid.reshape(blocks_here, BLOCKS, SPLIT, row_count),...  44.1 us
    all_to_all x1, waiting for transfers between devices, on_device(): lax.all_to_all(grad_first_out, 'block', split_axis=0, concat_axis=1, tile...  42.3 us
    div x1, other arithmetic, on_device(): adam_update = first_hat / (jnp.sqrt(second_hat) + 1e-08)  18 us
    dot_general x1, matrix products, on_device(): jnp.einsum('cjt,cfj->cft', grad_second, right_two, preferred_element_type...  16.6 us
    reshape x2, local copies, waits for them, and re-layouts, on_device(): first_mid.reshape(blocks_here, BLOCKS, SPLIT, row_count)  14.9 us
    reshape x2, local copies, waits for them, and re-layouts, on_device(): second_mid.reshape(blocks_here, BLOCKS, SPLIT, row_count)  14.9 us
  transfers between devices with their start and end apart: 8, of which 6 were waited for; matrix products, arithmetic and copies ran while one was open for 40% of the time, Pallas kernels for 0%

commit v1 on v0

--- a/solution.py
+++ b/solution.py
@@ -1,6 +1,11 @@
+import functools
+import math
+
 import jax
 import jax.numpy as jnp
 from jax import lax
+from jax.experimental import pallas as pl
+from jax.experimental.pallas import tpu as pltpu
 from jax.sharding import PartitionSpec as P
 
 BLOCKS = 96
@@ -9,12 +14,322 @@
 BLOCK_HID = 512
 MIDDLE = 384
 
+F32 = jnp.float32
+BF16 = jnp.bfloat16
+GROUP = 4
+LANES = 128
+VMEM_LIMIT = 48 * 1024 * 1024
+CHUNKS = (2, 4, 6)
+
+
+def dot(lhs, rhs, lhs_dim, rhs_dim):
+    return lax.dot_general(
+        lhs, rhs, (((lhs_dim,), (rhs_dim,)), ((), ())), preferred_element_type=F32
+    )
+
+
+def permutation(outer, inner):
+    size = outer * inner * SPLIT
+    row = lax.broadcasted_iota(jnp.int32, (size, size), 0)
+    col = lax.broadcasted_iota(jnp.int32, (size, size), 1)
+    at_outer = row // (inner * SPLIT)
+    at_inner = (row // SPLIT) % inner
+    source = at_inner * (outer * SPLIT) + at_outer * SPLIT + row % SPLIT
+    return jnp.where(col == source, 1.0, 0.0).astype(BF16)
+
+
+def first_kernel(chunks, ways, me_ref, x_ref, g_ref, right_ref, left_ref, *refs):
+    outs, (rows,) = refs[:-1], refs[-1:]
+    here = sum(chunks)
+    span = here * SPLIT
+    perm = permutation(here, GROUP)
+    for which in range(2):
+        for b in range(GROUP):
+            lanes = slice(b * BLOCK_IN, (b + 1) * BLOCK_IN)
+            if which == 0:
+                value = dot(right_ref[b], x_ref[:, lanes], 0, 1)
+            else:
+                value = dot(left_ref[b], g_ref[:, lanes], 1, 1)
+            rows[which, b] = value.astype(BF16)
+        for m in range(ways):
+            start = pl.multiple_of((me_ref[0] ^ m) * span, 16)
+            taken = jnp.concatenate(
+                [rows[which, b, pl.ds(start, span), :] for b in range(GROUP)], axis=0
+            )
+            mixed = dot(perm, taken, 1, 0).astype(BF16)
+            at = 0
+            for k, size in enumerate(chunks):
+                part = mixed[at * GROUP * SPLIT : (at + size) * GROUP * SPLIT]
+                outs[k * ways + m][which] = part.reshape(size, GROUP * SPLIT, part.shape[-1])
+                at += size
+
+
+def middle_kernel(ways, n_dp, scale, me_ref, *refs):
+    takes = refs[:ways]
+    left_ref, right_ref = refs[ways : ways + 2]
+    gives = refs[ways + 2 : 2 * ways + 2]
+    grads_ref = refs[2 * ways + 2]
+    first_in, grad_in, second_out, grad_out = refs[2 * ways + 3 :]
+    span = MIDDLE // ways
+    for m in range(ways):
+        start = pl.multiple_of((me_ref[0] ^ m) * span, 16)
+        first_in[pl.ds(start, span), :] = takes[m][0, 0]
+        grad_in[pl.ds(start, span), :] = takes[m][1, 0]
+    left = left_ref[0]
+    right = right_ref[0]
+    pre = dot(left, first_in[...], 0, 0)
+    root = math.sqrt(2.0 / math.pi)
+    square = pre * pre
+    bend = jnp.tanh(root * (pre + 0.044715 * (square * pre)))
+    half = 0.5 * (1.0 + bend)
+    hidden = (pre * half).astype(BF16)
+    slope = half + 0.5 * pre * (1.0 - bend * bend) * (root * (1.0 + 3 * 0.044715 * square))
+    second_out[...] = dot(right, hidden, 0, 0).astype(BF16)
+    grad_second = grad_in[...]
+    grad_pre = (dot(right, grad_second, 1, 0) * slope).astype(BF16)
+    grad_out[...] = dot(left, grad_pre, 1, 0).astype(BF16)
+    for m in range(ways):
+        start = pl.multiple_of((me_ref[0] ^ m) * span, 16)
+        gives[m][0, 0] = second_out[pl.ds(start, span), :]
+        gives[m][1, 0] = grad_out[pl.ds(start, span), :]
+    grad_right = (dot(hidden, grad_second, 1, 1) * scale).astype(BF16)
+    grad_left = (dot(first_in[...], grad_pre, 1, 1) * scale).astype(BF16)
+    at = 0
+    for grad in (grad_right, grad_left):
+        depth = grad.shape[0] // n_dp
+        for lane in range(0, grad.shape[1], LANES):
+            for z in range(n_dp):
+                grads_ref[z, 0, at : at + depth, :] = grad[
+                    z * depth : (z + 1) * depth, lane : lane + LANES
+                ]
+            at += depth
+
+
+def last_kernel(chunks, ways, n_dp, scale, me_ref, x_ref, g_ref, right_ref, *refs):
+    count = len(chunks) * ways
+    takes = refs[:count]
+    tokens_ref, grads_ref, rows = refs[count:]
+    here = sum(chunks)
+    span = here * SPLIT
+    perm = permutation(GROUP, here)
+    for which in range(2):
+        for m in range(ways):
+            start = pl.multiple_of((me_ref[0] ^ m) * span, 16)
+            taken = jnp.concatenate(
+                [
+                    takes[k * ways + m][which].reshape(size * GROUP * SPLIT, -1)
+                    for k, size in enumerate(chunks)
+                ],
+                axis=0,
+            )
+            mixed = dot(perm, taken, 1, 0).astype(BF16)
+            for b in range(GROUP):
+                rows[which, b, pl.ds(start, span), :] = mixed[b * span : (b + 1) * span]
+    for b in range(GROUP):
+        lanes = slice(b * BLOCK_IN, (b + 1) * BLOCK_IN)
+        second_in = rows[0, b]
+        grad_first = rows[1, b]
+        tokens_ref[:, lanes] = dot(grad_first, right_ref[b], 0, 1).astype(BF16)
+        grad_left = (dot(second_in, g_ref[:, lanes], 1, 0) * scale).astype(BF16)
+        grad_right = (dot(x_ref[:, lanes], grad_first, 0, 1) * scale).astype(BF16)
+        at = 0
+        for grad in (grad_left, grad_right):
+            depth = grad.shape[0] // n_dp
+            for lane in range(0, grad.shape[1], LANES):
+                for z in range(n_dp):
+                    grads_ref[z, b, at : at + depth, :] = grad[
+                        z * depth : (z + 1) * depth, lane : lane + LANES
+                    ]
+                at += depth
+
+
+def widen_kernel(n_old, sum_ref, *refs):
+    at = 0
+    for out_ref in refs[n_old:]:
+        depth, width = out_ref.shape[1:]
+        for lane in range(0, width, LANES):
+            out_ref[:, :, lane : lane + LANES] = sum_ref[0, :, at : at + depth, :].astype(F32)
+            at += depth
+
+
+def params():
+    return pltpu.CompilerParams(vmem_limit_bytes=VMEM_LIMIT)
+
+
+def cost(flops, moved, transcendentals=0):
+    return pl.CostEstimate(
+        flops=int(flops), bytes_accessed=int(moved), transcendentals=int(transcendentals)
+    )
+
+
+def widen(summed, shapes, here, first_block, old, per_step):
+    size, depth, _ = summed.shape[1:]
+    n_old = len(old)
+    any_spec = pl.BlockSpec(memory_space=pl.ANY)
+    at = first_block // per_step
+    return pl.pallas_call(
+        functools.partial(widen_kernel, n_old),
+        grid=(size // per_step,),
+        in_specs=[pl.BlockSpec((1, per_step, depth, LANES), lambda i: (0, i, 0, 0))]
+        + [any_spec] * n_old,
+        out_specs=[
+            pl.BlockSpec((per_step,) + tuple(shape), lambda i, at=at: (i + at, 0, 0))
+            for shape in shapes
+        ],
+        out_shape=[jax.ShapeDtypeStruct((here,) + tuple(shape), F32) for shape in shapes],
+        input_output_aliases={i + 1: i for i in range(n_old)},
+        compiler_params=params(),
+        cost_estimate=cost(0, summed.size * 6),
+        name="widen",
+    )(summed, *old)
+
+
+def on_device_fast(
+    tokens, cotangent, right_one, left_one, right_two, left_two, grad_prev, moment_one, moment_two
+):
+    rows = tokens.shape[0]
+    here = right_one.shape[0]
+    ways = lax.axis_size("block")
+    n_dp = lax.axis_size("dp")
+    span = here * SPLIT
+    scale = float(n_dp * rows) ** (-0.5)
+    me = lax.axis_index("block").astype(jnp.int32).reshape(1)
+    unit = here // sum(CHUNKS)
+    chunks = tuple(size * unit for size in CHUNKS)
+    n_groups = here // GROUP
+    tile = GROUP * SPLIT
+    wide = GROUP * BLOCK_IN
+
+    new_moment_one = 0.9 * moment_one + 0.1 * grad_prev
+    new_moment_two = 0.95 * moment_two + 0.05 * grad_prev * grad_prev
+    first_hat = new_moment_one / (1.0 - 0.9**10)
+    second_hat = new_moment_two / (1.0 - 0.95**10)
+    adam_update = first_hat / (jnp.sqrt(second_hat) + 1e-08)
+
+    token_spec = pl.BlockSpec((rows, wide), lambda i, me: (0, i))
+    right_spec = pl.BlockSpec((GROUP, BLOCK_IN, MIDDLE), lambda i, me: (i, 0, 0))
+    left_spec = pl.BlockSpec((GROUP, MIDDLE, BLOCK_IN), lambda i, me: (i, 0, 0))
+    part_specs = [
+        pl.BlockSpec((2, size, tile, rows), lambda i, me: (0, 0, i, 0))
+        for size in chunks
+        for _ in range(ways)
+    ]
+    part_shapes = [
+        jax.ShapeDtypeStruct((2, size, span, rows), BF16) for size in chunks for _ in range(ways)
+    ]
+    moved = 2 * here * MIDDLE * rows
+    sends = pl.pallas_call(
+        functools.partial(first_kernel, chunks, ways),
+        grid_spec=pltpu.PrefetchScalarGridSpec(
+            num_scalar_prefetch=1,
+            grid=(n_groups,),
+            in_specs=[token_spec, token_spec, right_spec, left_spec],
+            out_specs=part_specs,
+            scratch_shapes=[pltpu.VMEM((2, GROUP, MIDDLE, rows), BF16)],
+        ),
+        out_shape=part_shapes,
+        compiler_params=params(),
+        cost_estimate=cost(moved * BLOCK_IN * 5, 2 * moved),
+        name="first",
+    )(me, tokens, cotangent, right_one, left_two)
+
+    last_sent = [None] * ways
+
+    def exchange(parts):
+        got = [parts[0]]
+        for m in range(1, ways):
+            part = parts[m]
+            if last_sent[m] is not None:
+                part, _ = lax.optimization_barrier((part, last_sent[m]))
+            taken = lax.ppermute(part, "block", [(i, i ^ m) for i in range(ways)])
+            last_sent[m] = taken
+            got.append(taken)
+        return got
+
+    offsets = [sum(chunks[:k]) for k in range(len(chunks))]
+    arrived = [exchange(sends[k * ways : (k + 1) * ways]) for k in range(len(chunks))]
+
+    share = (BLOCK_HID * MIDDLE + MIDDLE * BLOCK_HID) // n_dp // LANES
+    middles = []
+    for k, size in enumerate(chunks):
+        at = offsets[k]
+        slice_spec = pl.BlockSpec((2, 1, span, rows), lambda i, me: (0, i, 0, 0))
+        flops = 12 * size * MIDDLE * BLOCK_HID * rows
+        outs = pl.pallas_call(
+            functools.partial(middle_kernel, ways, n_dp, scale),
+            grid_spec=pltpu.PrefetchScalarGridSpec(
+                num_scalar_prefetch=1,
+                grid=(size,),
+                in_specs=[slice_spec] * ways
+                + [
+                    pl.BlockSpec((1, MIDDLE, BLOCK_HID), lambda i, me, at=at: (i + at, 0, 0)),
+                    pl.BlockSpec((1, BLOCK_HID, MIDDLE), lambda i, me, at=at: (i + at, 0, 0)),
+                ],
+                out_specs=[slice_spec] * ways
+                + [pl.BlockSpec((n_dp, 1, share, LANES), lambda i, me: (0, i, 0, 0))],
+                scratch_shapes=[pltpu.VMEM((MIDDLE, rows), BF16)] * 4,
+            ),
+            out_shape=[jax.ShapeDtypeStruct((2, size, span, rows), BF16)] * ways
+            + [jax.ShapeDtypeStruct((n_dp, size, share, LANES), BF16)],
+            compiler_params=params(),
+            cost_estimate=cost(flops, size * MIDDLE * (8 * rows + 8 * BLOCK_HID)),
+            name="middle",
+        )(me, *arrived[k], left_one, right_two)
+        middles.append(outs)
+
+    def summed(grads):
+        return lax.psum_scatter(grads, "dp", scatter_dimension=0, tiled=True)
+
+    returned = [exchange(outs[:ways]) for outs in middles]
+    big_sums = [summed(outs[ways]) for outs in middles]
+
+    small_share = 2 * MIDDLE * BLOCK_IN // n_dp // LANES
+    grad_tokens, small_grads = pl.pallas_call(
+        functools.partial(last_kernel, chunks, ways, n_dp, scale),
+        grid_spec=pltpu.PrefetchScalarGridSpec(
+            num_scalar_prefetch=1,
+            grid=(n_groups,),
+            in_specs=[token_spec, token_spec, right_spec] + part_specs,
+            out_specs=[
+                token_spec,
+                pl.BlockSpec((n_dp, GROUP, small_share, LANES), lambda i, me: (0, i, 0, 0)),
+            ],
+            scratch_shapes=[pltpu.VMEM((2, GROUP, MIDDLE, rows), BF16)],
+        ),
+        out_shape=[
+            jax.ShapeDtypeStruct(tokens.shape, BF16),
+            jax.ShapeDtypeStruct((n_dp, here, small_share, LANES), BF16),
+        ],
+        compiler_params=params(),
+        cost_estimate=cost(moved * BLOCK_IN * 6, 2 * moved),
+        name="last",
+    )(me, tokens, cotangent, right_one, *[part for parts in returned for part in parts])
+    small_sum = summed(small_grads)
+
+    big_shapes = ((BLOCK_HID // n_dp, MIDDLE), (MIDDLE // n_dp, BLOCK_HID))
+    big = ()
+    for k, size in enumerate(chunks):
+        big = widen(big_sums[k], big_shapes, here, offsets[k], big, 1)
+    grad_right_two, grad_left_one = big
+    small_shapes = ((MIDDLE // n_dp, BLOCK_IN), (BLOCK_IN // n_dp, MIDDLE))
+    grad_left_two, grad_right_one = widen(small_sum, small_shapes, here, 0, (), GROUP)
+    return (
+        grad_tokens,
+        grad_right_one,
+        grad_left_one,
+        grad_right_two,
+        grad_left_two,
+        new_moment_one,
+        new_moment_two,
+        adam_update,
+    )
+
 
 def gelu_tanh(values):
     return jax.nn.gelu(values, approximate=True)
 
 
-def on_device(
+def on_device_plain(
     tokens, cotangent, right_one, left_one, right_two, left_two, grad_prev, moment_one, moment_two
 ):
     f32 = jnp.float32
@@ -134,6 +449,9 @@
         P("block", "dp"),
         P("block", "dp"),
     )
+    here = BLOCKS // mesh.shape["block"]
+    ways = mesh.shape["block"]
+    fits = here % sum(CHUNKS) == 0 and here % GROUP == 0 and ways & (ways - 1) == 0
     return jax.shard_map(
-        on_device, mesh=mesh, in_specs=in_specs, out_specs=out_specs, check_vma=False
-    )
+        on_device_fast if fits else on_device_plain, mesh=mesh, in_specs=in_specs, out_specs=out_specs, check_vma=False
+    )

time: 518 us -> 440 us (0.85); the launches traced: 509 us -> 440 us
  local copies, waits for them, and re-layouts: 124 us -> 14.4 us
  matrix products: 84.2 us -> 0 us
  Pallas kernels: 0 us -> 59.1 us
  waiting for transfers between devices: 241 us -> 289 us
  starting transfers between devices: 20.2 us -> 45.7 us
  other arithmetic: 25.7 us -> 17.8 us
    ppermute x0 -> x42, waiting for transfers between devices: none -> 178 us  [exchange(): taken = lax.ppermute(part, 'block', [(i, i ^ m) for i in range(ways)])]
    all_to_all x4 -> x0, waiting for transfers between devices: 93.4 us -> none  [the longest x1 44.1 us: on_device(): lax.all_to_all(first_mid.reshape(blocks_here, BLOCKS, SPLIT, row_count),...]
    dot_general x11 -> x0, matrix products: 84.2 us -> none  [the longest x1 16.6 us: on_device(): jnp.einsum('cjt,cfj->cft', grad_second, right_two, preferred_element_type...]
    pallas_call x0 -> x9, Pallas kernels: none -> 59.1 us  [the longest x3 32.8 us: on_device_fast(): pl.pallas_call(functools.partial(middle_kernel, ways, n_dp, scale), grid_...]
    reshape x7 -> x0, local copies, waits for them, and re-layouts: 53 us -> none  [the longest x2 14.9 us: on_device(): first_mid.reshape(blocks_here, BLOCKS, SPLIT, row_count)]
    ppermute x0 -> x42, starting transfers between devices: none -> 45.4 us  [exchange(): taken = lax.ppermute(part, 'block', [(i, i ^ m) for i in range(ways)])]
    reduce_scatter x4, waiting for transfers between devices: 147 us -> 111 us  [summed(): return lax.psum_scatter(grads, 'dp', scatter_dimension=0, tiled=True)]
    convert_element_type x6 -> x0, local copies, waits for them, and re-layouts: 32.3 us -> none  [the longest x2 13.8 us: on_device(): grad_left_one.astype(jnp.bfloat16)]
  transfers between devices with their start and end apart: 8 -> 46, of which waited for: 6 -> 22; matrix products, arithmetic and copies ran while one was open for 40% -> 4% of each run, Pallas kernels for 0% -> 9%
where the time goes in v1:
time: 440 us
  waiting for transfers between devices  289 us (66%)
  Pallas kernels  59.1 us (13%)
  starting transfers between devices  45.7 us (10%)
  other arithmetic  17.8 us (4%)
  local copies, waits for them, and re-layouts  14.4 us (3%)
  between operations  13.9 us (3%)
    ppermute x42, waiting for transfers between devices, exchange(): taken = lax.ppermute(part, 'block', [(i, i ^ m) for i in range(ways)])  178 us
    reduce_scatter x4, waiting for transfers between devices, summed(): return lax.psum_scatter(grads, 'dp', scatter_dimension=0, tiled=True)  111 us
    ppermute x42, starting transfers between devices, exchange(): taken = lax.ppermute(part, 'block', [(i, i ^ m) for i in range(ways)])  45.4 us
    pallas_call x3, Pallas kernels, on_device_fast(): pl.pallas_call(functools.partial(middle_kernel, ways, n_dp, scale), grid_...  32.8 us
    div x1, other arithmetic, on_device_fast(): adam_update = first_hat / (jnp.sqrt(second_hat) + 1e-08)  17.8 us
    unnamed x58, local copies, waits for them, and re-layouts  14.4 us
    pallas_call x1, Pallas kernels, on_device_fast(): pl.pallas_call(functools.partial(last_kernel, chunks, ways, n_dp, scale),...  10.1 us
    pallas_call x1, Pallas kernels, on_device_fast(): pl.pallas_call(functools.partial(first_kernel, chunks, ways), grid_spec=p...  9.64 us
  transfers between devices with their start and end apart: 46, of which 22 were waited for; matrix products, arithmetic and copies ran while one was open for 4% of the time, Pallas kernels for 9%

profile of v1, /device:TPU:0, one launch (start us, length us, event | category | flops | bytes accessed | tf_op | source)
XLA Modules:
  0.0 439.8 jit_solution(18051463666129082842)
XLA Ops:
  7.2 9.6 %first.1 = (bf16[2,2,48,512]{3,2,1,0:T(8,128)(2,1)S(1)}, bf16[2,2,48,512]{3,2,1,0:T(8,128)(2,1)S(1)}, bf16[2,2,48,512]{3,2,1,0:T(8,128)(2,1)S(1)}, bf16[2,2,48,5...) custom-call(s32[1]{0:T(128)} %bitcast.me_ref, ...), custom_call_target="tpu_custom_call" | custom-call | flops 3019898880 | bytes 9437184 | tf_op jit(solution)/shard_map/first/pallas_call | solution.py:221
  31.0 9.5 %collective-permute-done.4.refs_5_ = bf16[2,2,48,512]{3,2,1,0:T(8,128)(2,1)S(1)} collective-permute-done((bf16[2,2,48,512]{3,2,1,0:T(8,128)(2,1)S(1)}, bf16[2,2,48,512]{3,2,1,0:T(8,128)(2,1)S(1)}, u32[]{:S(2)}, u32[]{:S(2)}) %collective-permute-start.4) | collective-permute-done | bytes 196640 | tf_op jit(solution)/shard_map/ppermute | solution.py:244
  40.5 6.4 %middle.3 = (bf16[2,2,48,512]{3,2,1,0:T(8,128)(2,1)S(1)}, bf16[2,2,48,512]{3,2,1,0:T(8,128)(2,1)S(1)}, bf16[2,2,48,512]{3,2,1,0:T(8,128)(2,1)S(1)}, bf16[2,2,48,...) custom-call(s32[1]{0:T(128)} %bitcast.me_ref, ...), custom_call_target="tpu_custom_call" | custom-call | flops 2415919104 | bytes 6291456 | tf_op jit(solution)/shard_map/middle/pallas_call | solution.py:258
  51.7 2.9 collective-permute-start.25
  58.0 6.1 %collective-permute-done.25.refs_7_ = bf16[2,4,48,512]{3,2,1,0:T(8,128)(2,1)S(1)} collective-permute-done((bf16[2,4,48,512]{3,2,1,0:T(8,128)(2,1)S(1)}, bf16[2,4,48,512]{3,2,1,0:T(8,128)(2,1)S(1)}, u32[]{:S(2)}, u32[]{:S(2)}) %collective-permute-start.25) | collective-permute-done | bytes 393248 | tf_op jit(solution)/shard_map/ppermute | solution.py:244
  64.7 8.5 %collective-permute-done.22.refs_6_ = bf16[2,4,48,512]{3,2,1,0:T(8,128)(2,1)S(1)} collective-permute-done((bf16[2,4,48,512]{3,2,1,0:T(8,128)(2,1)S(1)}, bf16[2,4,48,512]{3,2,1,0:T(8,128)(2,1)S(1)}, u32[]{:S(2)}, u32[]{:S(2)}) %collective-permute-start.22) | collective-permute-done | bytes 393248 | tf_op jit(solution)/shard_map/ppermute | solution.py:244
  73.2 7.9 %collective-permute-done.19.refs_5_ = bf16[2,4,48,512]{3,2,1,0:T(8,128)(2,1)S(1)} collective-permute-done((bf16[2,4,48,512]{3,2,1,0:T(8,128)(2,1)S(1)}, bf16[2,4,48,512]{3,2,1,0:T(8,128)(2,1)S(1)}, u32[]{:S(2)}, u32[]{:S(2)}) %collective-permute-start.19) | collective-permute-done | bytes 393248 | tf_op jit(solution)/shard_map/ppermute | solution.py:244
  81.1 8.5 %collective-permute-done.16.refs_4_ = bf16[2,4,48,512]{3,2,1,0:T(8,128)(2,1)S(1)} collective-permute-done((bf16[2,4,48,512]{3,2,1,0:T(8,128)(2,1)S(1)}, bf16[2,4,48,512]{3,2,1,0:T(8,128)(2,1)S(1)}, u32[]{:S(2)}, u32[]{:S(2)}) %collective-permute-start.16) | collective-permute-done | bytes 393248 | tf_op jit(solution)/shard_map/ppermute | solution.py:244
  90.8 10.9 %middle.4 = (bf16[2,4,48,512]{3,2,1,0:T(8,128)(2,1)S(1)}, bf16[2,4,48,512]{3,2,1,0:T(8,128)(2,1)S(1)}, bf16[2,4,48,512]{3,2,1,0:T(8,128)(2,1)S(1)}, bf16[2,4,48,...) custom-call(s32[1]{0:T(128)} %bitcast.me_ref, ...), custom_call_target="tpu_custom_call" | custom-call | flops 4831838208 | bytes 12582912 | tf_op jit(solution)/shard_map/middle/pallas_call | solution.py:258
  105.2 14.2 %collective-permute-done.26.refs_7_ = bf16[2,6,48,512]{3,2,1,0:T(8,128)(2,1)S(1)} collective-permute-done((bf16[2,6,48,512]{3,2,1,0:T(8,128)(2,1)}, bf16[2,6,48,512]{3,2,1,0:T(8,128)(2,1)S(1)}, u32[]{:S(2)}, u32[]{:S(2)}) %collective-permute-start.26) | collective-permute-done | bytes 589856 | tf_op jit(solution)/shard_map/ppermute | solution.py:244
  122.6 9.7 %collective-permute-done.23.refs_6_ = bf16[2,6,48,512]{3,2,1,0:T(8,128)(2,1)S(1)} collective-permute-done((bf16[2,6,48,512]{3,2,1,0:T(8,128)(2,1)}, bf16[2,6,48,512]{3,2,1,0:T(8,128)(2,1)S(1)}, u32[]{:S(2)}, u32[]{:S(2)}) %collective-permute-start.23) | collective-permute-done | bytes 589856 | tf_op jit(solution)/shard_map/ppermute | solution.py:244
  132.2 2.6 collective-permute-start.24
  137.5 15.8 %collective-permute-done.24.refs_6_ = bf16[2,2,48,512]{3,2,1,0:T(8,128)(2,1)S(1)} collective-permute-done((bf16[2,2,48,512]{3,2,1,0:T(8,128)(2,1)}, bf16[2,2,48,512]{3,2,1,0:T(8,128)(2,1)S(1)}, u32[]{:S(2)}, u32[]{:S(2)}) %collective-permute-start.24) | collective-permute-done | bytes 196640 | tf_op jit(solution)/shard_map/ppermute | solution.py:244
  157.7 7.9 %collective-permute-done.14.refs_3_ = bf16[2,6,48,512]{3,2,1,0:T(8,128)(2,1)S(1)} collective-permute-done((bf16[2,6,48,512]{3,2,1,0:T(8,128)(2,1)}, bf16[2,6,48,512]{3,2,1,0:T(8,128)(2,1)S(1)}, u32[]{:S(2)}, u32[]{:S(2)}) %collective-permute-start.14) | collective-permute-done | bytes 589856 | tf_op jit(solution)/shard_map/ppermute | solution.py:244
  167.8 18.0 %collective-permute-done.20.refs_5_ = bf16[2,6,48,512]{3,2,1,0:T(8,128)(2,1)S(1)} collective-permute-done((bf16[2,6,48,512]{3,2,1,0:T(8,128)(2,1)}, bf16[2,6,48,512]{3,2,1,0:T(8,128)(2,1)S(1)}, u32[]{:S(2)}, u32[]{:S(2)}) %collective-permute-start.20) | collective-permute-done | bytes 589856 | tf_op jit(solution)/shard_map/ppermute | solution.py:244
  190.8 15.6 %middle.5 = (bf16[2,6,48,512]{3,2,1,0:T(8,128)(2,1)S(1)}, bf16[2,6,48,512]{3,2,1,0:T(8,128)(2,1)S(1)}, bf16[2,6,48,512]{3,2,1,0:T(8,128)(2,1)S(1)}, bf16[2,6,48,...) custom-call(s32[1]{0:T(128)} %bitcast.me_ref, ...), custom_call_target="tpu_custom_call" | custom-call | flops 7247757312 | bytes 18874368 | tf_op jit(solution)/shard_map/middle/pallas_call | solution.py:258
  212.1 31.2 %collective-permute-done.30.refs_11_ = bf16[2,4,48,512]{3,2,1,0:T(8,128)(2,1)S(1)} collective-permute-done((bf16[2,4,48,512]{3,2,1,0:T(8,128)(2,1)S(1)}, bf16[2,4,48,512]{3,2,1,0:T(8,128)(2,1)S(1)}, u32[]{:S(2)}, u32[]{:S(2)}) %collective-permute-start.30) | collective-permute-done | bytes 393248 | tf_op jit(solution)/shard_map/ppermute | solution.py:244
  244.0 8.4 %collective-permute-done.32.refs_13_ = bf16[2,4,48,512]{3,2,1,0:T(8,128)(2,1)S(1)} collective-permute-done((bf16[2,4,48,512]{3,2,1,0:T(8,128)(2,1)S(1)}, bf16[2,4,48,512]{3,2,1,0:T(8,128)(2,1)S(1)}, u32[]{:S(2)}, u32[]{:S(2)}) %collective-permute-start.32) | collective-permute-done | bytes 393248 | tf_op jit(solution)/shard_map/ppermute | solution.py:244
  256.0 11.7 %collective-permute-done.39.refs_21_ = bf16[2,6,48,512]{3,2,1,0:T(8,128)(2,1)S(1)} collective-permute-done((bf16[2,6,48,512]{3,2,1,0:T(8,128)(2,1)S(1)}, bf16[2,6,48,512]{3,2,1,0:T(8,128)(2,1)S(1)}, u32[]{:S(2)}, u32[]{:S(2)}) %collective-permute-start.39) | collective-permute-done | bytes 589856 | tf_op jit(solution)/shard_map/ppermute | solution.py:244
  267.7 12.9 %collective-permute-done.38.refs_20_ = bf16[2,6,48,512]{3,2,1,0:T(8,128)(2,1)S(1)} collective-permute-done((bf16[2,6,48,512]{3,2,1,0:T(8,128)(2,1)S(1)}, bf16[2,6,48,512]{3,2,1,0:T(8,128)(2,1)S(1)}, u32[]{:S(2)}, u32[]{:S(2)}) %collective-permute-start.38) | collective-permute-done | bytes 589856 | tf_op jit(solution)/shard_map/ppermute | solution.py:244
  283.2 10.1 %last.1 = (bf16[512,1536]{1,0:T(8,128)(2,1)}, bf16[4,12,192,128]{3,2,1,0:T(8,128)(2,1)}) custom-call(s32[1]{0:T(128)} %bitcast.me_ref, bf16[512,1536]{1,0:T(8,128)(2,1)} %x_ref.3, bf16[512,1536]{1,0:T(8,128)(2,1)} %g_ref.3, bf16[12,128,384]{2,1,0:T(8,128)(2,1)} %right_ref.3, bf16[2,2,48,512]{3,2,1,0:T(8,128)(2,1)S(1)} %get-tuple-element.112.refs_0_, ...), custom_call_target="tpu_custom_call" | custom-call | flops 3623878656 | bytes 9437184 | tf_op jit(solution)/shard_map/last/pallas_call | solution.py:287
  294.0 17.8 %add_divide_fusion = (f32[12,122880]{1,0:T(8,128)}, f32[12,122880]{1,0:T(8,128)}, f32[12,122880]{1,0:T(8,128)}) fusion(f32[12,122880]{1,0:T(8,128)} %param.15, f32[12,122880]{1,0:T(8,128)} %param.17, f32[12,122880]{1,0:T(8,128)} %param.16), kind=kLoop, calls=%fused_computation.2 | loop fusion | flops 16220160 | bytes 35389440 | tf_op jit(solution)/shard_map/div | solution.py:207
  316.4 26.2 %reduce-scatter.5.cloned.1.call-done.sum_ref = bf16[1,12,192,128]{3,2,1,0:T(8,128)(2,1)} async-done(((bf16[4,12,192,128]{3,2,1,0:T(8,128)(2,1)}), bf16[1,12,192,128]{3,2,1,0:T(8,128)(2,1)}) %reduce-scatter.5.cloned.1.call-update) | async-done | bytes 589840 | tf_op jit(solution)/shard_map/reduce_scatter | solution.py:281
  345.2 84.4 %reduce-scatter.7.cloned.1.call-done.sum_ref = bf16[1,6,768,128]{3,2,1,0:T(8,128)(2,1)} async-done(((bf16[4,6,768,128]{3,2,1,0:T(8,128)(2,1)}), bf16[1,6,768,128]{3,2,1,0:T(8,128)(2,1)}) %reduce-scatter.7.cloned.1.call-update) | async-done | bytes 1179664 | tf_op jit(solution)/shard_map/reduce_scatter | solution.py:281
  (140 shorter events, 69.1 us)
Async XLA Ops:
  7.2 304.6 %reduce-scatter.11.cloned.1.call-start = ((), (), s32[]{:S(2)}) async-start(), calls=%async_computation.7 | async-start | bytes 1966080 | tf_op jit(solution)/shard_map/reduce_scatter | solution.py:281
  51.6 262.0 %reduce-scatter.9.cloned.1.call-start = ((), (), s32[]{:S(2)}) async-start(), calls=%async_computation.6 | async-start | bytes 3932160 | tf_op jit(solution)/shard_map/reduce_scatter | solution.py:281
  54.9 26.3 %collective-permute-start.19 = (bf16[2,4,48,512]{3,2,1,0:T(8,128)(2,1)S(1)}, bf16[2,4,48,512]{3,2,1,0:T(8,128)(2,1)S(1)}, u32[]{:S(2)}, u32[]{:S(2)}) collective-permute-start(bf16[2,4,48,512]{3,2,1,0:T(8,128)(2,1)S(1)} %get-tuple-element.140), channel_id=1, source_target_pairs={{0,20},{4,16},{8,28},{12,24},{16,4},{20,0},{24,12},{28,8},{1,21},{... | collective-permute-start | bytes 1179656 | tf_op jit(solution)/shard_map/ppermute | solution.py:244
  56.0 33.6 %collective-permute-start.16 = (bf16[2,4,48,512]{3,2,1,0:T(8,128)(2,1)S(1)}, bf16[2,4,48,512]{3,2,1,0:T(8,128)(2,1)S(1)}, u32[]{:S(2)}, u32[]{:S(2)}) collective-permute-start(bf16[2,4,48,512]{3,2,1,0:T(8,128)(2,1)S(1)} %get-tuple-element.134), channel_id=1, source_target_pairs={{0,16},{4,20},{8,24},{12,28},{16,0},{20,4},{24,8},{28,12},{1,17},{... | collective-permute-start | bytes 1179656 | tf_op jit(solution)/shard_map/ppermute | solution.py:244
  56.6 32.9 %collective-permute-start.13 = (bf16[2,4,48,512]{3,2,1,0:T(8,128)(2,1)S(1)}, bf16[2,4,48,512]{3,2,1,0:T(8,128)(2,1)S(1)}, u32[]{:S(2)}, u32[]{:S(2)}) collective-permute-start(bf16[2,4,48,512]{3,2,1,0:T(8,128)(2,1)S(1)} %get-tuple-element.128), channel_id=1, source_target_pairs={{0,12},{4,8},{8,4},{12,0},{16,28},{20,24},{24,20},{28,16},{1,13},{... | collective-permute-start | bytes 1179656 | tf_op jit(solution)/shard_map/ppermute | solution.py:244
  102.5 240.2 %reduce-scatter.5.cloned.1.call-start = ((), (), s32[]{:S(2)}) async-start(), calls=%async_computation.4 | async-start | bytes 2949120 | tf_op jit(solution)/shard_map/reduce_scatter | solution.py:281
  104.9 27.4 %collective-permute-start.23 = (bf16[2,6,48,512]{3,2,1,0:T(8,128)(2,1)}, bf16[2,6,48,512]{3,2,1,0:T(8,128)(2,1)S(1)}, u32[]{:S(2)}, u32[]{:S(2)}) collective-permute-start(bf16[2,6,48,512]{3,2,1,0:T(8,128)(2,1)} %get-tuple-element.147), channel_id=1, source_target_pairs={{0,24},{4,28},{8,16},{12,20},{16,8},{20,12},{24,0},{28,4},{1,25},{... | collective-permute-start | bytes 1769480 | tf_op jit(solution)/shard_map/ppermute | solution.py:244
  122.0 32.2 %collective-permute-start.8 = (bf16[2,6,48,512]{3,2,1,0:T(8,128)(2,1)S(1)}, bf16[2,6,48,512]{3,2,1,0:T(8,128)(2,1)S(1)}, u32[]{:S(2)}, u32[]{:S(2)}) collective-permute-start(bf16[2,6,48,512]{3,2,1,0:T(8,128)(2,1)S(1)} %get-tuple-element.117), channel_id=1, source_target_pairs={{0,4},{4,0},{8,12},{12,8},{16,20},{20,16},{24,28},{28,24},{1,5},{5... | collective-permute-start | bytes 1769480 | tf_op jit(solution)/shard_map/ppermute | solution.py:244
  122.0 33.8 %collective-permute-start.11 = (bf16[2,6,48,512]{3,2,1,0:T(8,128)(2,1)}, bf16[2,6,48,512]{3,2,1,0:T(8,128)(2,1)S(1)}, u32[]{:S(2)}, u32[]{:S(2)}) collective-permute-start(bf16[2,6,48,512]{3,2,1,0:T(8,128)(2,1)} %get-tuple-element.123), channel_id=1, source_target_pairs={{0,8},{4,12},{8,0},{12,4},{16,24},{20,28},{24,16},{28,20},{1,9},{5... | collective-permute-start | bytes 1769480 | tf_op jit(solution)/shard_map/ppermute | solution.py:244
  134.8 30.7 %collective-permute-start.14 = (bf16[2,6,48,512]{3,2,1,0:T(8,128)(2,1)}, bf16[2,6,48,512]{3,2,1,0:T(8,128)(2,1)S(1)}, u32[]{:S(2)}, u32[]{:S(2)}) collective-permute-start(bf16[2,6,48,512]{3,2,1,0:T(8,128)(2,1)} %get-tuple-element.129), channel_id=1, source_target_pairs={{0,12},{4,8},{8,4},{12,0},{16,28},{20,24},{24,20},{28,16},{1,13},{... | collective-permute-start | bytes 1769480 | tf_op jit(solution)/shard_map/ppermute | solution.py:244
  136.3 30.0 %collective-permute-start.17 = (bf16[2,6,48,512]{3,2,1,0:T(8,128)(2,1)}, bf16[2,6,48,512]{3,2,1,0:T(8,128)(2,1)S(1)}, u32[]{:S(2)}, u32[]{:S(2)}) collective-permute-start(bf16[2,6,48,512]{3,2,1,0:T(8,128)(2,1)} %get-tuple-element.135), channel_id=1, source_target_pairs={{0,16},{4,20},{8,24},{12,28},{16,0},{20,4},{24,8},{28,12},{1,17},{... | collective-permute-start | bytes 1769480 | tf_op jit(solution)/shard_map/ppermute | solution.py:244
  153.4 32.5 %collective-permute-start.20 = (bf16[2,6,48,512]{3,2,1,0:T(8,128)(2,1)}, bf16[2,6,48,512]{3,2,1,0:T(8,128)(2,1)S(1)}, u32[]{:S(2)}, u32[]{:S(2)}) collective-permute-start(bf16[2,6,48,512]{3,2,1,0:T(8,128)(2,1)} %get-tuple-element.141), channel_id=1, source_target_pairs={{0,20},{4,16},{8,28},{12,24},{16,4},{20,0},{24,12},{28,8},{1,21},{... | collective-permute-start | bytes 1769480 | tf_op jit(solution)/shard_map/ppermute | solution.py:244
  154.2 34.6 %collective-permute-start.34 = (bf16[2,4,48,512]{3,2,1,0:T(8,128)(2,1)}, bf16[2,4,48,512]{3,2,1,0:T(8,128)(2,1)S(1)}, u32[]{:S(2)}, u32[]{:S(2)}) collective-permute-start(bf16[2,4,48,512]{3,2,1,0:T(8,128)(2,1)} %copy-done.4), channel_id=1, source_target_pairs={{0,28},{4,24},{8,20},{12,16},{16,12},{20,8},{24,4},{28,0},{1,29},{... | collective-permute-start | bytes 1179656 | tf_op jit(solution)/shard_map/ppermute | solution.py:244
  155.8 33.5 %collective-permute-start.33 = (bf16[2,4,48,512]{3,2,1,0:T(8,128)(2,1)S(1)}, bf16[2,4,48,512]{3,2,1,0:T(8,128)(2,1)S(1)}, u32[]{:S(2)}, u32[]{:S(2)}) collective-permute-start(bf16[2,4,48,512]{3,2,1,0:T(8,128)(2,1)S(1)} %get-tuple-element.168), channel_id=1, source_target_pairs={{0,24},{4,28},{8,16},{12,20},{16,8},{20,12},{24,0},{28,4},{1,25},{... | collective-permute-start | bytes 1179656 | tf_op jit(solution)/shard_map/ppermute | solution.py:244
  206.3 48.9 %collective-permute-start.41 = (bf16[2,6,48,512]{3,2,1,0:T(8,128)(2,1)S(1)}, bf16[2,6,48,512]{3,2,1,0:T(8,128)(2,1)S(1)}, u32[]{:S(2)}, u32[]{:S(2)}) collective-permute-start(bf16[2,6,48,512]{3,2,1,0:T(8,128)(2,1)S(1)} %get-tuple-element.186), channel_id=1, source_target_pairs={{0,28},{4,24},{8,20},{12,16},{16,12},{20,8},{24,4},{28,0},{1,29},{... | collective-permute-start | bytes 1769480 | tf_op jit(solution)/shard_map/ppermute | solution.py:244
  208.8 47.1 %collective-permute-start.40 = (bf16[2,6,48,512]{3,2,1,0:T(8,128)(2,1)S(1)}, bf16[2,6,48,512]{3,2,1,0:T(8,128)(2,1)S(1)}, u32[]{:S(2)}, u32[]{:S(2)}) collective-permute-start(bf16[2,6,48,512]{3,2,1,0:T(8,128)(2,1)S(1)} %get-tuple-element.184), channel_id=1, source_target_pairs={{0,24},{4,28},{8,16},{12,20},{16,8},{20,12},{24,0},{28,4},{1,25},{... | collective-permute-start | bytes 1769480 | tf_op jit(solution)/shard_map/ppermute | solution.py:244
  209.1 34.2 %collective-permute-start.30 = (bf16[2,4,48,512]{3,2,1,0:T(8,128)(2,1)S(1)}, bf16[2,4,48,512]{3,2,1,0:T(8,128)(2,1)S(1)}, u32[]{:S(2)}, u32[]{:S(2)}) collective-permute-start(bf16[2,4,48,512]{3,2,1,0:T(8,128)(2,1)S(1)} %get-tuple-element.162), channel_id=1, source_target_pairs={{0,12},{4,8},{8,4},{12,0},{16,28},{20,24},{24,20},{28,16},{1,13},{... | collective-permute-start | bytes 1179656 | tf_op jit(solution)/shard_map/ppermute | solution.py:244
  210.1 33.9 %collective-permute-start.31 = (bf16[2,4,48,512]{3,2,1,0:T(8,128)(2,1)S(1)}, bf16[2,4,48,512]{3,2,1,0:T(8,128)(2,1)S(1)}, u32[]{:S(2)}, u32[]{:S(2)}) collective-permute-start(bf16[2,4,48,512]{3,2,1,0:T(8,128)(2,1)S(1)} %get-tuple-element.164), channel_id=1, source_target_pairs={{0,16},{4,20},{8,24},{12,28},{16,0},{20,4},{24,8},{28,12},{1,17},{... | collective-permute-start | bytes 1179656 | tf_op jit(solution)/shard_map/ppermute | solution.py:244
  211.7 40.7 %collective-permute-start.32 = (bf16[2,4,48,512]{3,2,1,0:T(8,128)(2,1)S(1)}, bf16[2,4,48,512]{3,2,1,0:T(8,128)(2,1)S(1)}, u32[]{:S(2)}, u32[]{:S(2)}) collective-permute-start(bf16[2,4,48,512]{3,2,1,0:T(8,128)(2,1)S(1)} %get-tuple-element.166), channel_id=1, source_target_pairs={{0,20},{4,16},{8,28},{12,24},{16,4},{20,0},{24,12},{28,8},{1,21},{... | collective-permute-start | bytes 1179656 | tf_op jit(solution)/shard_map/ppermute | solution.py:244
  253.5 27.2 %collective-permute-start.38 = (bf16[2,6,48,512]{3,2,1,0:T(8,128)(2,1)S(1)}, bf16[2,6,48,512]{3,2,1,0:T(8,128)(2,1)S(1)}, u32[]{:S(2)}, u32[]{:S(2)}) collective-permute-start(bf16[2,6,48,512]{3,2,1,0:T(8,128)(2,1)S(1)} %get-tuple-element.180), channel_id=1, source_target_pairs={{0,16},{4,20},{8,24},{12,28},{16,0},{20,4},{24,8},{28,12},{1,17},{... | collective-permute-start | bytes 1769480 | tf_op jit(solution)/shard_map/ppermute | solution.py:244
  254.1 26.5 %collective-permute-start.37 = (bf16[2,6,48,512]{3,2,1,0:T(8,128)(2,1)S(1)}, bf16[2,6,48,512]{3,2,1,0:T(8,128)(2,1)S(1)}, u32[]{:S(2)}, u32[]{:S(2)}) collective-permute-start(bf16[2,6,48,512]{3,2,1,0:T(8,128)(2,1)S(1)} %get-tuple-element.178), channel_id=1, source_target_pairs={{0,12},{4,8},{8,4},{12,0},{16,28},{20,24},{24,20},{28,16},{1,13},{... | collective-permute-start | bytes 1769480 | tf_op jit(solution)/shard_map/ppermute | solution.py:244
  255.2 27.2 %collective-permute-start.36 = (bf16[2,6,48,512]{3,2,1,0:T(8,128)(2,1)S(1)}, bf16[2,6,48,512]{3,2,1,0:T(8,128)(2,1)S(1)}, u32[]{:S(2)}, u32[]{:S(2)}) collective-permute-start(bf16[2,6,48,512]{3,2,1,0:T(8,128)(2,1)S(1)} %get-tuple-element.176), channel_id=1, source_target_pairs={{0,8},{4,12},{8,0},{12,4},{16,24},{20,28},{24,16},{28,20},{1,9},{5... | collective-permute-start | bytes 1769480 | tf_op jit(solution)/shard_map/ppermute | solution.py:244
  256.0 26.5 %collective-permute-start.35 = (bf16[2,6,48,512]{3,2,1,0:T(8,128)(2,1)S(1)}, bf16[2,6,48,512]{3,2,1,0:T(8,128)(2,1)S(1)}, u32[]{:S(2)}, u32[]{:S(2)}) collective-permute-start(bf16[2,6,48,512]{3,2,1,0:T(8,128)(2,1)S(1)} %get-tuple-element.174), channel_id=1, source_target_pairs={{0,4},{4,0},{8,12},{12,8},{16,20},{20,16},{24,28},{28,24},{1,5},{5... | collective-permute-start | bytes 1769480 | tf_op jit(solution)/shard_map/ppermute | solution.py:244
  293.4 136.2 %reduce-scatter.7.cloned.1.call-start = ((), (), s32[]{:S(2)}) async-start(), calls=%async_computation.5 | async-start | bytes 5898240 | tf_op jit(solution)/shard_map/reduce_scatter | solution.py:281
  (51 other events, 698.4 us)
Sparse Core Ops, SparseCore 0:
  51.8 36.9 reduce-scatter.10
  102.6 61.4 reduce-scatter.8
  293.5 49.1 reduce-scatter.4
  344.8 84.7 reduce-scatter.6

commit v2 on v1

--- a/solution.py
+++ b/solution.py
@@ -18,7 +18,7 @@
 BF16 = jnp.bfloat16
 GROUP = 4
 LANES = 128
-VMEM_LIMIT = 48 * 1024 * 1024
+VMEM_LIMIT = 62 * 1024 * 1024
 CHUNKS = (2, 4, 6)
 
 
@@ -152,6 +152,10 @@
             at += depth
 
 
+def in_hbm(arrays):
+    return [pltpu.with_memory_space_constraint(array, pltpu.HBM) for array in arrays]
+
+
 def params():
     return pltpu.CompilerParams(vmem_limit_bytes=VMEM_LIMIT)
 
@@ -215,7 +219,7 @@
         for _ in range(ways)
     ]
     part_shapes = [
-        jax.ShapeDtypeStruct((2, size, span, rows), BF16) for size in chunks for _ in range(ways)
+        pltpu.HBM((2, size, span, rows), BF16) for size in chunks for _ in range(ways)
     ]
     moved = 2 * here * MIDDLE * rows
     sends = pl.pallas_call(
@@ -233,29 +237,24 @@
         name="first",
     )(me, tokens, cotangent, right_one, left_two)
 
-    last_sent = [None] * ways
-
-    def exchange(parts):
-        got = [parts[0]]
-        for m in range(1, ways):
-            part = parts[m]
-            if last_sent[m] is not None:
-                part, _ = lax.optimization_barrier((part, last_sent[m]))
-            taken = lax.ppermute(part, "block", [(i, i ^ m) for i in range(ways)])
-            last_sent[m] = taken
-            got.append(taken)
-        return got
-
+    def permute(parts, ms):
+        return {m: lax.ppermute(parts[m], "block", [(i, i ^ m) for i in range(ways)]) for m in ms}
+
+    def after(arrays, *done):
+        held = lax.optimization_barrier((arrays, done))
+        return held[0]
+
+    early = [m for m in range(1, ways) if m & (m - 1) == 0 and m > 1]
+    late = [m for m in range(1, ways) if m not in early]
     offsets = [sum(chunks[:k]) for k in range(len(chunks))]
-    arrived = [exchange(sends[k * ways : (k + 1) * ways]) for k in range(len(chunks))]
+    n_parts = len(chunks)
 
     share = (BLOCK_HID * MIDDLE + MIDDLE * BLOCK_HID) // n_dp // LANES
-    middles = []
-    for k, size in enumerate(chunks):
-        at = offsets[k]
+    def middle(k, takes):
+        size, at = chunks[k], offsets[k]
         slice_spec = pl.BlockSpec((2, 1, span, rows), lambda i, me: (0, i, 0, 0))
         flops = 12 * size * MIDDLE * BLOCK_HID * rows
-        outs = pl.pallas_call(
+        return pl.pallas_call(
             functools.partial(middle_kernel, ways, n_dp, scale),
             grid_spec=pltpu.PrefetchScalarGridSpec(
                 num_scalar_prefetch=1,
@@ -269,19 +268,43 @@
                 + [pl.BlockSpec((n_dp, 1, share, LANES), lambda i, me: (0, i, 0, 0))],
                 scratch_shapes=[pltpu.VMEM((MIDDLE, rows), BF16)] * 4,
             ),
-            out_shape=[jax.ShapeDtypeStruct((2, size, span, rows), BF16)] * ways
-            + [jax.ShapeDtypeStruct((n_dp, size, share, LANES), BF16)],
+            out_shape=[pltpu.HBM((2, size, span, rows), BF16)] * ways
+            + [pltpu.HBM((n_dp, size, share, LANES), BF16)],
             compiler_params=params(),
             cost_estimate=cost(flops, size * MIDDLE * (8 * rows + 8 * BLOCK_HID)),
             name="middle",
-        )(me, *arrived[k], left_one, right_two)
-        middles.append(outs)
+        )(me, *in_hbm(takes), left_one, right_two)
 
     def summed(grads):
         return lax.psum_scatter(grads, "dp", scatter_dimension=0, tiled=True)
 
-    returned = [exchange(outs[:ways]) for outs in middles]
-    big_sums = [summed(outs[ways]) for outs in middles]
+    queue = [dict(enumerate(sends[k * ways : (k + 1) * ways])) for k in range(n_parts)]
+    got = [{0: parts[0]} for parts in queue]
+    got[0].update(permute(queue[0], range(1, ways)))
+    middles, big_sums = [], []
+    for k in range(n_parts):
+        parts = queue[k + 1] if k + 1 < n_parts else dict(enumerate(middles[0][:ways]))
+        if k + 1 == n_parts:
+            got.append({0: parts[0]})
+        takes, ahead = lax.optimization_barrier((got[k], {m: parts[m] for m in early}))
+        outs = middle(k, [takes[m] for m in range(ways)])
+        ahead = permute(ahead, early)
+        ahead, outs = lax.optimization_barrier((ahead, tuple(outs)))
+        rest = after({m: parts[m] for m in late}, ahead)
+        got[k + 1].update(ahead)
+        got[k + 1].update(permute(rest, late))
+        middles.append(outs)
+        big_sums.append(summed(outs[ways]))
+    returned = [got[n_parts]]
+    for k in range(1, n_parts):
+        parts = dict(enumerate(middles[k][:ways]))
+        parts, _ = lax.optimization_barrier((parts, big_sums[k - 1]))
+        before = returned[-1]
+        taken = {0: parts[0]}
+        for m in range(1, ways):
+            taken.update(permute({m: after(parts[m], before[m])}, [m]))
+        returned.append(taken)
+    returned = [[taken[m] for m in range(ways)] for taken in returned]
 
     small_share = 2 * MIDDLE * BLOCK_IN // n_dp // LANES
     grad_tokens, small_grads = pl.pallas_call(
@@ -298,12 +321,13 @@
         ),
         out_shape=[
             jax.ShapeDtypeStruct(tokens.shape, BF16),
-            jax.ShapeDtypeStruct((n_dp, here, small_share, LANES), BF16),
+            pltpu.HBM((n_dp, here, small_share, LANES), BF16),
         ],
         compiler_params=params(),
         cost_estimate=cost(moved * BLOCK_IN * 6, 2 * moved),
         name="last",
-    )(me, tokens, cotangent, right_one, *[part for parts in returned for part in parts])
+    )(me, tokens, cotangent, right_one, *in_hbm([part for parts in returned for part in parts]))
+    small_grads, _ = lax.optimization_barrier((small_grads, big_sums[-1]))
     small_sum = summed(small_grads)
 
     big_shapes = ((BLOCK_HID // n_dp, MIDDLE), (MIDDLE // n_dp, BLOCK_HID))

time: 440 us -> 339 us (0.77)
  waiting for transfers between devices: 289 us -> 192 us
  local copies, waits for them, and re-layouts: 14.4 us -> 0.45 us
  Pallas kernels: 59.1 us -> 67.3 us
    reduce_scatter x4, waiting for transfers between devices: 111 us -> 21.2 us  [summed(): return lax.psum_scatter(grads, 'dp', scatter_dimension=0, tiled=True)]
    unnamed x58 -> x80, local copies, waits for them, and re-layouts: 14.4 us -> 0.45 us
    ppermute x42, waiting for transfers between devices: 178 us -> 171 us  [permute(): lax.ppermute(parts[m], 'block', [(i, i ^ m) for i in range(ways)])]
    pallas_call x4, Pallas kernels: 6.45 us -> 12.7 us  [widen(): pl.pallas_call(functools.partial(widen_kernel, n_old), grid=(size // per_...]
  transfers between devices with their start and end apart: 46 -> 46, of which waited for: 22 -> 22; matrix products, arithmetic and copies ran while one was open for 4% -> 5% of each run, Pallas kernels for 9% -> 16%
where the time goes in v2:
time: 339 us; the launch traced here: 338 us
  waiting for transfers between devices  192 us (57%)
  Pallas kernels  67.3 us (20%)
  starting transfers between devices  46.7 us (14%)
  other arithmetic  17.8 us (5%)
  between operations  14.1 us (4%)
    ppermute x42, waiting for transfers between devices, permute(): lax.ppermute(parts[m], 'block', [(i, i ^ m) for i in range(ways)])  171 us
    ppermute x42, starting transfers between devices, permute(): lax.ppermute(parts[m], 'block', [(i, i ^ m) for i in range(ways)])  46.4 us
    pallas_call x3, Pallas kernels, middle(): pl.pallas_call(functools.partial(middle_kernel, ways, n_dp, scale), grid_...  33.8 us
    reduce_scatter x4, waiting for transfers between devices, summed(): return lax.psum_scatter(grads, 'dp', scatter_dimension=0, tiled=True)  21.2 us
    div x1, other arithmetic, on_device_fast(): adam_update = first_hat / (jnp.sqrt(second_hat) + 1e-08)  17.8 us
    pallas_call x4, Pallas kernels, widen(): pl.pallas_call(functools.partial(widen_kernel, n_old), grid=(size // per_...  12.7 us
    pallas_call x1, Pallas kernels, on_device_fast(): pl.pallas_call(functools.partial(last_kernel, chunks, ways, n_dp, scale),...  10.8 us
    pallas_call x1, Pallas kernels, on_device_fast(): pl.pallas_call(functools.partial(first_kernel, chunks, ways), grid_spec=p...  9.98 us
  transfers between devices with their start and end apart: 46, of which 22 were waited for; matrix products, arithmetic and copies ran while one was open for 5% of the time, Pallas kernels for 16%

profile of v2, /device:TPU:0, one launch (start us, length us, event | category | flops | bytes accessed | tf_op | source)
XLA Modules:
  0.0 338.4 jit_solution(1440290692002202898)
XLA Ops:
  7.2 10.0 %first.1 = (bf16[2,2,48,512]{3,2,1,0:T(8,128)(2,1)}, bf16[2,2,48,512]{3,2,1,0:T(8,128)(2,1)}, bf16[2,2,48,512]{3,2,1,0:T(8,128)(2,1)}, bf16[2,2,48,512]{3,2,1,0:...) custom-call(s32[1]{0:T(128)} %bitcast.me_ref, ...), custom_call_target="tpu_custom_call" | custom-call | flops 3019898880 | bytes 9437184 | tf_op jit(solution)/shard_map/first/pallas_call | solution.py:225
  17.7 2.6 collective-permute-start.1
  22.1 2.6 collective-permute-start.5
  30.1 9.7 %collective-permute-done.4.refs_5_ = bf16[2,2,48,512]{3,2,1,0:T(8,128)(2,1)S(1)} collective-permute-done((bf16[2,2,48,512]{3,2,1,0:T(8,128)(2,1)}, bf16[2,2,48,512]{3,2,1,0:T(8,128)(2,1)S(1)}, u32[]{:S(2)}, u32[]{:S(2)}) %collective-permute-start.4) | collective-permute-done | bytes 196640 | tf_op jit(solution)/shard_map/ppermute | solution.py:241
  43.2 6.9 %middle.3 = (bf16[2,2,48,512]{3,2,1,0:T(8,128)(2,1)}, bf16[2,2,48,512]{3,2,1,0:T(8,128)(2,1)}, bf16[2,2,48,512]{3,2,1,0:T(8,128)(2,1)}, bf16[2,2,48,512]{3,2,1,0...) custom-call(s32[1]{0:T(128)} %bitcast.me_ref, ...), custom_call_target="tpu_custom_call" | custom-call | flops 2415919104 | bytes 6291456 | tf_op jit(solution)/shard_map/middle/pallas_call | solution.py:257
  57.8 6.6 %collective-permute-done.10.refs_3_ = bf16[2,4,48,512]{3,2,1,0:T(8,128)(2,1)S(1)} collective-permute-done((bf16[2,4,48,512]{3,2,1,0:T(8,128)(2,1)}, bf16[2,4,48,512]{3,2,1,0:T(8,128)(2,1)S(1)}, u32[]{:S(2)}, u32[]{:S(2)}) %collective-permute-start.10) | collective-permute-done | bytes 393248 | tf_op jit(solution)/shard_map/ppermute | solution.py:241
  64.4 17.2 %collective-permute-done.11.refs_5_ = bf16[2,4,48,512]{3,2,1,0:T(8,128)(2,1)S(1)} collective-permute-done((bf16[2,4,48,512]{3,2,1,0:T(8,128)(2,1)}, bf16[2,4,48,512]{3,2,1,0:T(8,128)(2,1)S(1)}, u32[]{:S(2)}, u32[]{:S(2)}) %collective-permute-start.11) | collective-permute-done | bytes 393248 | tf_op jit(solution)/shard_map/ppermute | solution.py:241
  85.4 11.3 %middle.4 = (bf16[2,4,48,512]{3,2,1,0:T(8,128)(2,1)}, bf16[2,4,48,512]{3,2,1,0:T(8,128)(2,1)}, bf16[2,4,48,512]{3,2,1,0:T(8,128)(2,1)}, bf16[2,4,48,512]{3,2,1,0...) custom-call(s32[1]{0:T(128)} %bitcast.me_ref, ...), custom_call_target="tpu_custom_call" | custom-call | flops 4831838208 | bytes 12582912 | tf_op jit(solution)/shard_map/middle/pallas_call | solution.py:257
  104.8 10.2 %collective-permute-done.17.refs_3_ = bf16[2,6,48,512]{3,2,1,0:T(8,128)(2,1)S(1)} collective-permute-done((bf16[2,6,48,512]{3,2,1,0:T(8,128)(2,1)}, bf16[2,6,48,512]{3,2,1,0:T(8,128)(2,1)S(1)}, u32[]{:S(2)}, u32[]{:S(2)}) %collective-permute-start.17) | collective-permute-done | bytes 589856 | tf_op jit(solution)/shard_map/ppermute | solution.py:241
  115.1 25.8 %collective-permute-done.18.refs_5_ = bf16[2,6,48,512]{3,2,1,0:T(8,128)(2,1)S(1)} collective-permute-done((bf16[2,6,48,512]{3,2,1,0:T(8,128)(2,1)S(1)}, bf16[2,6,48,512]{3,2,1,0:T(8,128)(2,1)S(1)}, u32[]{:S(2)}, u32[]{:S(2)}) %collective-permute-start.18) | collective-permute-done | bytes 589856 | tf_op jit(solution)/shard_map/ppermute | solution.py:241
  144.4 15.7 %middle.5 = (bf16[2,6,48,512]{3,2,1,0:T(8,128)(2,1)}, bf16[2,6,48,512]{3,2,1,0:T(8,128)(2,1)}, bf16[2,6,48,512]{3,2,1,0:T(8,128)(2,1)}, bf16[2,6,48,512]{3,2,1,0...) custom-call(s32[1]{0:T(128)} %bitcast.me_ref, ...), custom_call_target="tpu_custom_call" | custom-call | flops 7247757312 | bytes 18874368 | tf_op jit(solution)/shard_map/middle/pallas_call | solution.py:257
  164.2 4.7 %collective-permute-done.27.refs_7_ = bf16[2,2,48,512]{3,2,1,0:T(8,128)(2,1)S(1)} collective-permute-done((bf16[2,2,48,512]{3,2,1,0:T(8,128)(2,1)}, bf16[2,2,48,512]{3,2,1,0:T(8,128)(2,1)S(1)}, u32[]{:S(2)}, u32[]{:S(2)}) %collective-permute-start.27) | collective-permute-done | bytes 196640 | tf_op jit(solution)/shard_map/ppermute | solution.py:241
  170.9 11.0 %collective-permute-done.26.refs_6_ = bf16[2,2,48,512]{3,2,1,0:T(8,128)(2,1)} collective-permute-done((bf16[2,2,48,512]{3,2,1,0:T(8,128)(2,1)S(1)}, bf16[2,2,48,512]{3,2,1,0:T(8,128)(2,1)}, u32[]{:S(2)}, u32[]{:S(2)}) %collective-permute-start.26) | collective-permute-done | bytes 196640 | tf_op jit(solution)/shard_map/ppermute | solution.py:241
  185.3 17.7 %collective-permute-done.24.refs_3_ = bf16[2,2,48,512]{3,2,1,0:T(8,128)(2,1)S(1)} collective-permute-done((bf16[2,2,48,512]{3,2,1,0:T(8,128)(2,1)}, bf16[2,2,48,512]{3,2,1,0:T(8,128)(2,1)S(1)}, u32[]{:S(2)}, u32[]{:S(2)}) %collective-permute-start.24) | collective-permute-done | bytes 196640 | tf_op jit(solution)/shard_map/ppermute | solution.py:241
  207.0 20.0 %collective-permute-done.32.refs_13_ = bf16[2,4,48,512]{3,2,1,0:T(8,128)(2,1)S(1)} collective-permute-done((bf16[2,4,48,512]{3,2,1,0:T(8,128)(2,1)}, bf16[2,4,48,512]{3,2,1,0:T(8,128)(2,1)S(1)}, u32[]{:S(2)}, u32[]{:S(2)}) %collective-permute-start.32) | collective-permute-done | bytes 393248 | tf_op jit(solution)/shard_map/ppermute | solution.py:241
  232.0 11.9 %collective-permute-done.37.refs_19_ = bf16[2,6,48,512]{3,2,1,0:T(8,128)(2,1)} collective-permute-done((bf16[2,6,48,512]{3,2,1,0:T(8,128)(2,1)}, bf16[2,6,48,512]{3,2,1,0:T(8,128)(2,1)}, u32[]{:S(2)}, u32[]{:S(2)}) %collective-permute-start.37) | collective-permute-done | bytes 589856 | tf_op jit(solution)/shard_map/ppermute | solution.py:241
  244.6 12.7 %collective-permute-done.40.refs_22_ = bf16[2,6,48,512]{3,2,1,0:T(8,128)(2,1)} collective-permute-done((bf16[2,6,48,512]{3,2,1,0:T(8,128)(2,1)}, bf16[2,6,48,512]{3,2,1,0:T(8,128)(2,1)}, u32[]{:S(2)}, u32[]{:S(2)}) %collective-permute-start.40) | collective-permute-done | bytes 589856 | tf_op jit(solution)/shard_map/ppermute | solution.py:241
  257.3 12.1 %collective-permute-done.41.refs_23_ = bf16[2,6,48,512]{3,2,1,0:T(8,128)(2,1)} collective-permute-done((bf16[2,6,48,512]{3,2,1,0:T(8,128)(2,1)}, bf16[2,6,48,512]{3,2,1,0:T(8,128)(2,1)}, u32[]{:S(2)}, u32[]{:S(2)}) %collective-permute-start.41) | collective-permute-done | bytes 589856 | tf_op jit(solution)/shard_map/ppermute | solution.py:241
  269.5 10.8 %last.1 = (bf16[512,1536]{1,0:T(8,128)(2,1)}, bf16[4,12,192,128]{3,2,1,0:T(8,128)(2,1)}) custom-call(s32[1]{0:T(128)} %bitcast.me_ref, bf16[512,1536]{1,0:T(8,128)(2,1)} %x_ref.3, bf16[512,1536]{1,0:T(8,128)(2,1)} %g_ref.3, bf16[12,128,384]{2,1,0:T(8,128)(2,1)} %right_ref.3, bf16[2,2,48,512]{3,2,1,0:T(8,128)(2,1)} %get-tuple-element.207.refs_0_, ...), custom_call_target="tpu_custom_call" | custom-call | flops 3623878656 | bytes 9437184 | tf_op jit(solution)/shard_map/last/pallas_call | solution.py:310
  280.3 17.8 %add_divide_fusion = (f32[12,122880]{1,0:T(8,128)}, f32[12,122880]{1,0:T(8,128)}, f32[12,122880]{1,0:T(8,128)}) fusion(f32[12,122880]{1,0:T(8,128)} %param.15, f32[12,122880]{1,0:T(8,128)} %param.17, f32[12,122880]{1,0:T(8,128)} %param.16), kind=kLoop, calls=%fused_computation.2 | loop fusion | flops 16220160 | bytes 35389440 | tf_op jit(solution)/shard_map/div | solution.py:211
  299.9 3.4 %widen.6 = (f32[12,128,384]{2,1,0:T(8,128)}, f32[12,96,512]{2,1,0:T(8,128)}) custom-call(bf16[1,4,768,128]{3,2,1,0:T(8,128)(2,1)} %reduce-scatter.7.cloned.1.call-done.sum_ref, f32[12,128,384]{2,1,0:T(8,128)} %get-tuple-element.341.refs_0_, f32[12,96,512]{2,1,0:T(8,128)} %get-tuple-element.342.refs_1_), custom_call_target="tpu_custom_call", output_to_operand_aliasing={{0}: (1, {}), {1}: (2, {})} | custom-call | bytes 2359296 | tf_op jit(solution)/shard_map/widen/pallas_call | solution.py:174
  303.3 4.6 %widen.7 = (f32[12,128,384]{2,1,0:T(8,128)}, f32[12,96,512]{2,1,0:T(8,128)}) custom-call(bf16[1,6,768,128]{3,2,1,0:T(8,128)(2,1)} %reduce-scatter.9.cloned.1.call-done.sum_ref, f32[12,128,384]{2,1,0:T(8,128)} %get-tuple-element.343.refs_0_, f32[12,96,512]{2,1,0:T(8,128)} %get-tuple-element.344.refs_1_), custom_call_target="tpu_custom_call", output_to_operand_aliasing={{0}: (1, {}), {1}: (2, {})} | custom-call | bytes 3538944 | tf_op jit(solution)/shard_map/widen/pallas_call | solution.py:174
  307.9 21.1 %reduce-scatter.11.cloned.1.call-done.sum_ref = bf16[1,12,192,128]{3,2,1,0:T(8,128)(2,1)} async-done(((bf16[4,12,192,128]{3,2,1,0:T(8,128)(2,1)}), bf16[1,12,192,128]{3,2,1,0:T(8,128)(2,1)}) %reduce-scatter.11.cloned.1.call-update) | async-done | bytes 589840 | tf_op jit(solution)/shard_map/reduce_scatter | solution.py:279
  329.0 2.9 widen.4
  (162 shorter events, 55.2 us)
Async XLA Ops:
  7.2 153.2 %reduce-scatter.5.cloned.1.call-start = ((), (), s32[]{:S(2)}) async-start(), calls=%async_computation.4 | async-start | bytes 1966080 | tf_op jit(solution)/shard_map/reduce_scatter | solution.py:279
  53.1 132.2 %reduce-scatter.7.cloned.1.call-start = ((), (), s32[]{:S(2)}) async-start(), calls=%async_computation.5 | async-start | bytes 3932160 | tf_op jit(solution)/shard_map/reduce_scatter | solution.py:279
  53.7 27.8 %collective-permute-start.11 = (bf16[2,4,48,512]{3,2,1,0:T(8,128)(2,1)}, bf16[2,4,48,512]{3,2,1,0:T(8,128)(2,1)S(1)}, u32[]{:S(2)}, u32[]{:S(2)}) collective-permute-start(bf16[2,4,48,512]{3,2,1,0:T(8,128)(2,1)} %get-tuple-element.229), channel_id=1, source_target_pairs={{0,20},{4,16},{8,28},{12,24},{16,4},{20,0},{24,12},{28,8},{1,21},{... | collective-permute-start | bytes 1179656 | tf_op jit(solution)/shard_map/ppermute | solution.py:241
  55.1 26.5 %collective-permute-start.12 = (bf16[2,4,48,512]{3,2,1,0:T(8,128)(2,1)}, bf16[2,4,48,512]{3,2,1,0:T(8,128)(2,1)S(1)}, u32[]{:S(2)}, u32[]{:S(2)}) collective-permute-start(bf16[2,4,48,512]{3,2,1,0:T(8,128)(2,1)} %get-tuple-element.230), channel_id=1, source_target_pairs={{0,24},{4,28},{8,16},{12,20},{16,8},{20,12},{24,0},{28,4},{1,25},{... | collective-permute-start | bytes 1179656 | tf_op jit(solution)/shard_map/ppermute | solution.py:241
  56.5 25.6 %collective-permute-start.13 = (bf16[2,4,48,512]{3,2,1,0:T(8,128)(2,1)S(1)}, bf16[2,4,48,512]{3,2,1,0:T(8,128)(2,1)S(1)}, u32[]{:S(2)}, u32[]{:S(2)}) collective-permute-start(bf16[2,4,48,512]{3,2,1,0:T(8,128)(2,1)S(1)} %copy-done.32), channel_id=1, source_target_pairs={{0,28},{4,24},{8,20},{12,16},{16,12},{20,8},{24,4},{28,0},{1,29},{... | collective-permute-start | bytes 1179656 | tf_op jit(solution)/shard_map/ppermute | solution.py:241
  99.6 180.7 %reduce-scatter.9.cloned.1.call-start = ((), (), s32[]{:S(2)}) async-start(), calls=%async_computation.6 | async-start | bytes 5898240 | tf_op jit(solution)/shard_map/reduce_scatter | solution.py:279
  100.9 39.9 %collective-permute-start.18 = (bf16[2,6,48,512]{3,2,1,0:T(8,128)(2,1)S(1)}, bf16[2,6,48,512]{3,2,1,0:T(8,128)(2,1)S(1)}, u32[]{:S(2)}, u32[]{:S(2)}) collective-permute-start(bf16[2,6,48,512]{3,2,1,0:T(8,128)(2,1)S(1)} %copy-done.23), channel_id=1, source_target_pairs={{0,20},{4,16},{8,28},{12,24},{16,4},{20,0},{24,12},{28,8},{1,21},{... | collective-permute-start | bytes 1769480 | tf_op jit(solution)/shard_map/ppermute | solution.py:241
  102.1 38.8 %collective-permute-start.19 = (bf16[2,6,48,512]{3,2,1,0:T(8,128)(2,1)S(1)}, bf16[2,6,48,512]{3,2,1,0:T(8,128)(2,1)S(1)}, u32[]{:S(2)}, u32[]{:S(2)}) collective-permute-start(bf16[2,6,48,512]{3,2,1,0:T(8,128)(2,1)S(1)} %copy-done.22), channel_id=1, source_target_pairs={{0,24},{4,28},{8,16},{12,20},{16,8},{20,12},{24,0},{28,4},{1,25},{... | collective-permute-start | bytes 1769480 | tf_op jit(solution)/shard_map/ppermute | solution.py:241
  103.0 38.3 %collective-permute-start.20 = (bf16[2,6,48,512]{3,2,1,0:T(8,128)(2,1)S(1)}, bf16[2,6,48,512]{3,2,1,0:T(8,128)(2,1)S(1)}, u32[]{:S(2)}, u32[]{:S(2)}) collective-permute-start(bf16[2,6,48,512]{3,2,1,0:T(8,128)(2,1)S(1)} %copy-done.21), channel_id=1, source_target_pairs={{0,28},{4,24},{8,20},{12,16},{16,12},{20,8},{24,4},{28,0},{1,29},{... | collective-permute-start | bytes 1769480 | tf_op jit(solution)/shard_map/ppermute | solution.py:241
  160.1 168.9 %reduce-scatter.11.cloned.1.call-start = ((), (), s32[]{:S(2)}) async-start(), calls=%async_computation.7 | async-start | bytes 2949120 | tf_op jit(solution)/shard_map/reduce_scatter | solution.py:279
  160.4 24.0 %collective-permute-start.31 = (bf16[2,4,48,512]{3,2,1,0:T(8,128)(2,1)S(1)}, bf16[2,4,48,512]{3,2,1,0:T(8,128)(2,1)}, u32[]{:S(2)}, u32[]{:S(2)}) collective-permute-start(bf16[2,4,48,512]{3,2,1,0:T(8,128)(2,1)S(1)} %copy-done.31), channel_id=1, source_target_pairs={{0,16},{4,20},{8,24},{12,28},{16,0},{20,4},{24,8},{28,12},{1,17},{... | collective-permute-start | bytes 1179656 | tf_op jit(solution)/shard_map/ppermute | solution.py:241
  162.4 22.8 %collective-permute-start.29 = (bf16[2,4,48,512]{3,2,1,0:T(8,128)(2,1)S(1)}, bf16[2,4,48,512]{3,2,1,0:T(8,128)(2,1)}, u32[]{:S(2)}, u32[]{:S(2)}) collective-permute-start(bf16[2,4,48,512]{3,2,1,0:T(8,128)(2,1)S(1)} %copy-done.30), channel_id=1, source_target_pairs={{0,8},{4,12},{8,0},{12,4},{16,24},{20,28},{24,16},{28,20},{1,9},{5... | collective-permute-start | bytes 1179656 | tf_op jit(solution)/shard_map/ppermute | solution.py:241
  168.9 36.6 %collective-permute-start.34 = (bf16[2,4,48,512]{3,2,1,0:T(8,128)(2,1)}, bf16[2,4,48,512]{3,2,1,0:T(8,128)(2,1)S(1)}, u32[]{:S(2)}, u32[]{:S(2)}) collective-permute-start(bf16[2,4,48,512]{3,2,1,0:T(8,128)(2,1)} %get-tuple-element.311), channel_id=1, source_target_pairs={{0,28},{4,24},{8,20},{12,16},{16,12},{20,8},{24,4},{28,0},{1,29},{... | collective-permute-start | bytes 1179656 | tf_op jit(solution)/shard_map/ppermute | solution.py:241
  182.0 24.9 %collective-permute-start.33 = (bf16[2,4,48,512]{3,2,1,0:T(8,128)(2,1)}, bf16[2,4,48,512]{3,2,1,0:T(8,128)(2,1)S(1)}, u32[]{:S(2)}, u32[]{:S(2)}) collective-permute-start(bf16[2,4,48,512]{3,2,1,0:T(8,128)(2,1)} %get-tuple-element.309), channel_id=1, source_target_pairs={{0,24},{4,28},{8,16},{12,20},{16,8},{20,12},{24,0},{28,4},{1,25},{... | collective-permute-start | bytes 1179656 | tf_op jit(solution)/shard_map/ppermute | solution.py:241
  184.1 19.0 %collective-permute-start.24 = (bf16[2,2,48,512]{3,2,1,0:T(8,128)(2,1)}, bf16[2,2,48,512]{3,2,1,0:T(8,128)(2,1)S(1)}, u32[]{:S(2)}, u32[]{:S(2)}) collective-permute-start(bf16[2,2,48,512]{3,2,1,0:T(8,128)(2,1)} %get-tuple-element.284), channel_id=1, source_target_pairs={{0,12},{4,8},{8,4},{12,0},{16,28},{20,24},{24,20},{28,16},{1,13},{... | collective-permute-start | bytes 589832 | tf_op jit(solution)/shard_map/ppermute | solution.py:241
  184.4 19.7 %collective-permute-start.25 = (bf16[2,2,48,512]{3,2,1,0:T(8,128)(2,1)S(1)}, bf16[2,2,48,512]{3,2,1,0:T(8,128)(2,1)S(1)}, u32[]{:S(2)}, u32[]{:S(2)}) collective-permute-start(bf16[2,2,48,512]{3,2,1,0:T(8,128)(2,1)S(1)} %copy-done.38), channel_id=1, source_target_pairs={{0,20},{4,16},{8,28},{12,24},{16,4},{20,0},{24,12},{28,8},{1,21},{... | collective-permute-start | bytes 589832 | tf_op jit(solution)/shard_map/ppermute | solution.py:241
  185.2 19.6 %collective-permute-start.23 = (bf16[2,2,48,512]{3,2,1,0:T(8,128)(2,1)}, bf16[2,2,48,512]{3,2,1,0:T(8,128)(2,1)S(1)}, u32[]{:S(2)}, u32[]{:S(2)}) collective-permute-start(bf16[2,2,48,512]{3,2,1,0:T(8,128)(2,1)} %get-tuple-element.283), channel_id=1, source_target_pairs={{0,4},{4,0},{8,12},{12,8},{16,20},{20,16},{24,28},{28,24},{1,5},{5... | collective-permute-start | bytes 589832 | tf_op jit(solution)/shard_map/ppermute | solution.py:241
  203.0 26.6 %collective-permute-start.36 = (bf16[2,6,48,512]{3,2,1,0:T(8,128)(2,1)}, bf16[2,6,48,512]{3,2,1,0:T(8,128)(2,1)S(1)}, u32[]{:S(2)}, u32[]{:S(2)}) collective-permute-start(bf16[2,6,48,512]{3,2,1,0:T(8,128)(2,1)} %get-tuple-element.325), channel_id=1, source_target_pairs={{0,8},{4,12},{8,0},{12,4},{16,24},{20,28},{24,16},{28,20},{1,9},{5... | collective-permute-start | bytes 1769480 | tf_op jit(solution)/shard_map/ppermute | solution.py:241
  204.1 27.4 %collective-permute-start.38 = (bf16[2,6,48,512]{3,2,1,0:T(8,128)(2,1)}, bf16[2,6,48,512]{3,2,1,0:T(8,128)(2,1)S(1)}, u32[]{:S(2)}, u32[]{:S(2)}) collective-permute-start(bf16[2,6,48,512]{3,2,1,0:T(8,128)(2,1)} %get-tuple-element.329), channel_id=1, source_target_pairs={{0,16},{4,20},{8,24},{12,28},{16,0},{20,4},{24,8},{28,12},{1,17},{... | collective-permute-start | bytes 1769480 | tf_op jit(solution)/shard_map/ppermute | solution.py:241
  204.8 22.2 %collective-permute-start.32 = (bf16[2,4,48,512]{3,2,1,0:T(8,128)(2,1)}, bf16[2,4,48,512]{3,2,1,0:T(8,128)(2,1)S(1)}, u32[]{:S(2)}, u32[]{:S(2)}) collective-permute-start(bf16[2,4,48,512]{3,2,1,0:T(8,128)(2,1)} %get-tuple-element.307), channel_id=1, source_target_pairs={{0,20},{4,16},{8,28},{12,24},{16,4},{20,0},{24,12},{28,8},{1,21},{... | collective-permute-start | bytes 1179656 | tf_op jit(solution)/shard_map/ppermute | solution.py:241
  205.5 21.5 %collective-permute-start.30 = (bf16[2,4,48,512]{3,2,1,0:T(8,128)(2,1)}, bf16[2,4,48,512]{3,2,1,0:T(8,128)(2,1)S(1)}, u32[]{:S(2)}, u32[]{:S(2)}) collective-permute-start(bf16[2,4,48,512]{3,2,1,0:T(8,128)(2,1)} %get-tuple-element.303), channel_id=1, source_target_pairs={{0,12},{4,8},{8,4},{12,0},{16,28},{20,24},{24,20},{28,16},{1,13},{... | collective-permute-start | bytes 1179656 | tf_op jit(solution)/shard_map/ppermute | solution.py:241
  206.9 20.1 %collective-permute-start.28 = (bf16[2,4,48,512]{3,2,1,0:T(8,128)(2,1)S(1)}, bf16[2,4,48,512]{3,2,1,0:T(8,128)(2,1)S(1)}, u32[]{:S(2)}, u32[]{:S(2)}) collective-permute-start(bf16[2,4,48,512]{3,2,1,0:T(8,128)(2,1)S(1)} %copy-done.29), channel_id=1, source_target_pairs={{0,4},{4,0},{8,12},{12,8},{16,20},{20,16},{24,28},{28,24},{1,5},{5... | collective-permute-start | bytes 1179656 | tf_op jit(solution)/shard_map/ppermute | solution.py:241
  229.7 27.6 %collective-permute-start.40 = (bf16[2,6,48,512]{3,2,1,0:T(8,128)(2,1)}, bf16[2,6,48,512]{3,2,1,0:T(8,128)(2,1)}, u32[]{:S(2)}, u32[]{:S(2)}) collective-permute-start(bf16[2,6,48,512]{3,2,1,0:T(8,128)(2,1)} %get-tuple-element.333), channel_id=1, source_target_pairs={{0,24},{4,28},{8,16},{12,20},{16,8},{20,12},{24,0},{28,4},{1,25},{... | collective-permute-start | bytes 1769480 | tf_op jit(solution)/shard_map/ppermute | solution.py:241
  231.5 38.0 %collective-permute-start.41 = (bf16[2,6,48,512]{3,2,1,0:T(8,128)(2,1)}, bf16[2,6,48,512]{3,2,1,0:T(8,128)(2,1)}, u32[]{:S(2)}, u32[]{:S(2)}) collective-permute-start(bf16[2,6,48,512]{3,2,1,0:T(8,128)(2,1)} %get-tuple-element.335), channel_id=1, source_target_pairs={{0,28},{4,24},{8,20},{12,16},{16,12},{20,8},{24,4},{28,0},{1,29},{... | collective-permute-start | bytes 1769480 | tf_op jit(solution)/shard_map/ppermute | solution.py:241
  (62 other events, 1196.2 us)
Sparse Core Ops, SparseCore 0:
  53.2 35.5 reduce-scatter.4
  99.7 61.0 reduce-scatter.6
  163.7 85.2 reduce-scatter.8
  280.4 48.5 reduce-scatter.10

commit v3 on v2

--- a/solution.py
+++ b/solution.py
@@ -3,6 +3,7 @@
 
 import jax
 import jax.numpy as jnp
+import numpy as np
 from jax import lax
 from jax.experimental import pallas as pl
 from jax.experimental.pallas import tpu as pltpu
@@ -28,21 +29,20 @@
     )
 
 
+def one_hot(source, width):
+    return jnp.asarray(np.asarray(source)[:, None] == np.arange(width), dtype=BF16)
+
+
 def permutation(outer, inner):
-    size = outer * inner * SPLIT
-    row = lax.broadcasted_iota(jnp.int32, (size, size), 0)
-    col = lax.broadcasted_iota(jnp.int32, (size, size), 1)
-    at_outer = row // (inner * SPLIT)
-    at_inner = (row // SPLIT) % inner
-    source = at_inner * (outer * SPLIT) + at_outer * SPLIT + row % SPLIT
-    return jnp.where(col == source, 1.0, 0.0).astype(BF16)
-
-
-def first_kernel(chunks, ways, me_ref, x_ref, g_ref, right_ref, left_ref, *refs):
+    rows = np.arange(inner * outer * SPLIT).reshape(inner, outer, SPLIT)
+    return one_hot(rows.transpose(1, 0, 2).reshape(-1), rows.size)
+
+
+def first_kernel(chunks, ways, me_ref, x_ref, g_ref, right_ref, left_ref, perm_ref, *refs):
     outs, (rows,) = refs[:-1], refs[-1:]
     here = sum(chunks)
     span = here * SPLIT
-    perm = permutation(here, GROUP)
+    perm = perm_ref[...]
     for which in range(2):
         for b in range(GROUP):
             lanes = slice(b * BLOCK_IN, (b + 1) * BLOCK_IN)
@@ -57,19 +57,43 @@
                 [rows[which, b, pl.ds(start, span), :] for b in range(GROUP)], axis=0
             )
             mixed = dot(perm, taken, 1, 0).astype(BF16)
-            at = 0
-            for k, size in enumerate(chunks):
+            at = chunks[0]
+            for k, size in enumerate(chunks[1:]):
                 part = mixed[at * GROUP * SPLIT : (at + size) * GROUP * SPLIT]
                 outs[k * ways + m][which] = part.reshape(size, GROUP * SPLIT, part.shape[-1])
                 at += size
 
 
-def middle_kernel(ways, n_dp, scale, me_ref, *refs):
+def lead_kernel(size, ways, me_ref, x_ref, g_ref, right_ref, left_ref, perm_ref, pick_ref, *refs):
+    outs, rows = refs[:-1], refs[-1]
+    perm = perm_ref[...]
+    pick = pick_ref[...]
+    right = right_ref[...].reshape(GROUP * BLOCK_IN, MIDDLE)
+    right = dot(right, pick, 1, 1).astype(BF16)
+    left = [dot(pick, left_ref[b], 1, 0).astype(BF16) for b in range(GROUP)]
+    for which in range(2):
+        values = []
+        for b in range(GROUP):
+            lanes = slice(b * BLOCK_IN, (b + 1) * BLOCK_IN)
+            if which == 0:
+                value = dot(right[lanes], x_ref[:, lanes], 0, 1)
+            else:
+                value = dot(left[b], g_ref[:, lanes], 1, 1)
+            values.append(value.astype(BF16))
+        rows[...] = dot(perm, jnp.concatenate(values, axis=0), 1, 0).astype(BF16)
+        tall = size * GROUP * SPLIT
+        for m in range(ways):
+            start = pl.multiple_of((me_ref[0] ^ m) * tall, 16)
+            part = rows[pl.ds(start, tall), :]
+            outs[m][which] = part.reshape(size, GROUP * SPLIT, part.shape[-1])
+
+
+def middle_kernel(ways, n_old, n_dp, scale, me_ref, *refs):
     takes = refs[:ways]
     left_ref, right_ref = refs[ways : ways + 2]
-    gives = refs[ways + 2 : 2 * ways + 2]
-    grads_ref = refs[2 * ways + 2]
-    first_in, grad_in, second_out, grad_out = refs[2 * ways + 3 :]
+    refs = refs[ways + 2 + n_old :]
+    gives = refs[:ways]
+    grads_ref, first_in, grad_in, second_out, grad_out = refs[ways:]
     span = MIDDLE // ways
     for m in range(ways):
         start = pl.multiple_of((me_ref[0] ^ m) * span, 16)
@@ -105,13 +129,13 @@
             at += depth
 
 
-def last_kernel(chunks, ways, n_dp, scale, me_ref, x_ref, g_ref, right_ref, *refs):
+def last_kernel(chunks, ways, n_dp, scale, me_ref, x_ref, g_ref, right_ref, perm_ref, *refs):
     count = len(chunks) * ways
     takes = refs[:count]
     tokens_ref, grads_ref, rows = refs[count:]
     here = sum(chunks)
     span = here * SPLIT
-    perm = permutation(GROUP, here)
+    perm = perm_ref[...]
     for which in range(2):
         for m in range(ways):
             start = pl.multiple_of((me_ref[0] ^ m) * span, 16)
@@ -222,97 +246,155 @@
         pltpu.HBM((2, size, span, rows), BF16) for size in chunks for _ in range(ways)
     ]
     moved = 2 * here * MIDDLE * rows
-    sends = pl.pallas_call(
-        functools.partial(first_kernel, chunks, ways),
+    first_in_specs = [token_spec, token_spec, right_spec, left_spec]
+    lead_perm = permutation(ways * chunks[0], GROUP)
+    lead_rows = np.arange(MIDDLE).reshape(ways, here, SPLIT)[:, : chunks[0]]
+    lead_pick = one_hot(lead_rows.reshape(-1), MIDDLE)
+
+    def whole(array):
+        return pl.BlockSpec(array.shape, lambda i, me: (0, 0))
+
+    perm = permutation(here, GROUP)
+    perm_back = permutation(GROUP, here)
+    lead = pl.pallas_call(
+        functools.partial(lead_kernel, chunks[0], ways),
         grid_spec=pltpu.PrefetchScalarGridSpec(
             num_scalar_prefetch=1,
             grid=(n_groups,),
-            in_specs=[token_spec, token_spec, right_spec, left_spec],
-            out_specs=part_specs,
-            scratch_shapes=[pltpu.VMEM((2, GROUP, MIDDLE, rows), BF16)],
+            in_specs=first_in_specs + [whole(lead_perm), whole(lead_pick)],
+            out_specs=part_specs[:ways],
+            scratch_shapes=[pltpu.VMEM((ways * chunks[0] * tile, rows), BF16)],
         ),
-        out_shape=part_shapes,
+        out_shape=part_shapes[:ways],
         compiler_params=params(),
-        cost_estimate=cost(moved * BLOCK_IN * 5, 2 * moved),
-        name="first",
-    )(me, tokens, cotangent, right_one, left_two)
-
-    def permute(parts, ms):
-        return {m: lax.ppermute(parts[m], "block", [(i, i ^ m) for i in range(ways)]) for m in ms}
-
-    def after(arrays, *done):
-        held = lax.optimization_barrier((arrays, done))
-        return held[0]
-
-    early = [m for m in range(1, ways) if m & (m - 1) == 0 and m > 1]
-    late = [m for m in range(1, ways) if m not in early]
+        cost_estimate=cost(moved * BLOCK_IN * chunks[0] / here * 5, moved),
+        name="lead",
+    )(me, tokens, cotangent, right_one, left_two, lead_perm, lead_pick)
+
+    lane_done = {}
+
+    def send(parts, m):
+        part = parts[m]
+        if m // 2 in lane_done:
+            part, _ = lax.optimization_barrier((part, lane_done[m // 2]))
+        taken = lax.ppermute(part, "block", [(i, i ^ m) for i in range(ways)])
+        lane_done[m // 2] = taken
+        return taken
+
+    def send_all(parts, ms):
+        return {m: send(parts, m) for m in ms}
+
+    evens = list(range(2, ways, 2))
+    odds = list(range(1, ways, 2))
+    near = [m for m in range(2, ways) if (m // 2) & (m // 2 - 1) == 0]
+    everyone = evens + odds
     offsets = [sum(chunks[:k]) for k in range(len(chunks))]
     n_parts = len(chunks)
 
     share = (BLOCK_HID * MIDDLE + MIDDLE * BLOCK_HID) // n_dp // LANES
-    def middle(k, takes):
+    def middle(k, takes, old, first_give, n_give):
         size, at = chunks[k], offsets[k]
         slice_spec = pl.BlockSpec((2, 1, span, rows), lambda i, me: (0, i, 0, 0))
+        give_spec = pl.BlockSpec((2, 1, span, rows), lambda i, me: (0, i + first_give, 0, 0))
         flops = 12 * size * MIDDLE * BLOCK_HID * rows
         return pl.pallas_call(
-            functools.partial(middle_kernel, ways, n_dp, scale),
+            functools.partial(middle_kernel, ways, len(old), n_dp, scale),
             grid_spec=pltpu.PrefetchScalarGridSpec(
                 num_scalar_prefetch=1,
                 grid=(size,),
                 in_specs=[slice_spec] * ways
                 + [
-                    pl.BlockSpec((1, MIDDLE, BLOCK_HID), lambda i, me, at=at: (i + at, 0, 0)),
-                    pl.BlockSpec((1, BLOCK_HID, MIDDLE), lambda i, me, at=at: (i + at, 0, 0)),
-                ],
-                out_specs=[slice_spec] * ways
+                    pl.BlockSpec((1, MIDDLE, BLOCK_HID), lambda i, me: (i + at, 0, 0)),
+                    pl.BlockSpec((1, BLOCK_HID, MIDDLE), lambda i, me: (i + at, 0, 0)),
+                ]
+                + [pl.BlockSpec(memory_space=pl.ANY)] * len(old),
+                out_specs=[give_spec] * ways
                 + [pl.BlockSpec((n_dp, 1, share, LANES), lambda i, me: (0, i, 0, 0))],
                 scratch_shapes=[pltpu.VMEM((MIDDLE, rows), BF16)] * 4,
             ),
-            out_shape=[pltpu.HBM((2, size, span, rows), BF16)] * ways
+            out_shape=[pltpu.HBM((2, n_give, span, rows), BF16)] * ways
             + [pltpu.HBM((n_dp, size, share, LANES), BF16)],
+            input_output_aliases={ways + 3 + i: i for i in range(len(old))},
             compiler_params=params(),
             cost_estimate=cost(flops, size * MIDDLE * (8 * rows + 8 * BLOCK_HID)),
             name="middle",
-        )(me, *in_hbm(takes), left_one, right_two)
+        )(me, *in_hbm(takes), left_one, right_two, *in_hbm(old))
 
     def summed(grads):
         return lax.psum_scatter(grads, "dp", scatter_dimension=0, tiled=True)
 
-    queue = [dict(enumerate(sends[k * ways : (k + 1) * ways])) for k in range(n_parts)]
-    got = [{0: parts[0]} for parts in queue]
-    got[0].update(permute(queue[0], range(1, ways)))
-    middles, big_sums = [], []
-    for k in range(n_parts):
-        parts = queue[k + 1] if k + 1 < n_parts else dict(enumerate(middles[0][:ways]))
-        if k + 1 == n_parts:
-            got.append({0: parts[0]})
-        takes, ahead = lax.optimization_barrier((got[k], {m: parts[m] for m in early}))
-        outs = middle(k, [takes[m] for m in range(ways)])
-        ahead = permute(ahead, early)
-        ahead, outs = lax.optimization_barrier((ahead, tuple(outs)))
-        rest = after({m: parts[m] for m in late}, ahead)
-        got[k + 1].update(ahead)
-        got[k + 1].update(permute(rest, late))
-        middles.append(outs)
-        big_sums.append(summed(outs[ways]))
-    returned = [got[n_parts]]
-    for k in range(1, n_parts):
-        parts = dict(enumerate(middles[k][:ways]))
-        parts, _ = lax.optimization_barrier((parts, big_sums[k - 1]))
-        before = returned[-1]
-        taken = {0: parts[0]}
-        for m in range(1, ways):
-            taken.update(permute({m: after(parts[m], before[m])}, [m]))
-        returned.append(taken)
-    returned = [[taken[m] for m in range(ways)] for taken in returned]
-
-    small_share = 2 * MIDDLE * BLOCK_IN // n_dp // LANES
-    grad_tokens, small_grads = pl.pallas_call(
-        functools.partial(last_kernel, chunks, ways, n_dp, scale),
+    queue = [dict(enumerate(lead))]
+    got = [{0: lead[0]}]
+    for m in near + [m for m in everyone if m not in near]:
+        got[0][m] = lax.ppermute(lead[m], "block", [(i, i ^ m) for i in range(ways)])
+        lane_done[m // 2] = got[0][m]
+    rest = pl.pallas_call(
+        functools.partial(first_kernel, chunks, ways),
         grid_spec=pltpu.PrefetchScalarGridSpec(
             num_scalar_prefetch=1,
             grid=(n_groups,),
-            in_specs=[token_spec, token_spec, right_spec] + part_specs,
+            in_specs=first_in_specs + [whole(perm)],
+            out_specs=part_specs[ways:],
+            scratch_shapes=[pltpu.VMEM((2, GROUP, MIDDLE, rows), BF16)],
+        ),
+        out_shape=part_shapes[ways:],
+        compiler_params=params(),
+        cost_estimate=cost(moved * BLOCK_IN * 5, 2 * moved),
+        name="first",
+    )(me, tokens, cotangent, right_one, left_two, perm)
+    for k in range(n_parts - 1):
+        queue.append(dict(enumerate(rest[k * ways : (k + 1) * ways])))
+
+    early_size = offsets[-1]
+    back_chunks = (early_size, chunks[-1])
+    big_sums, early, held = [], (), {}
+    for k in range(n_parts):
+        last_part = k + 1 == n_parts
+        if last_part:
+            parts = dict(enumerate(early))
+            ahead = send_all(parts, [m for m in near if m % 2 == 0] + [m for m in near if m % 2])
+            outs = middle(k, [got[k][m] for m in range(ways)], (), 0, chunks[-1])
+        else:
+            parts = queue[k + 1]
+            ahead = send_all(parts, [m for m in near if m % 2 == 0])
+            outs = middle(k, [got[k][m] for m in range(ways)], early, offsets[k], early_size)
+        held, outs = lax.optimization_barrier((ahead, tuple(outs)))
+        big_sums.append(summed(outs[ways]))
+        parts = lax.optimization_barrier((parts, held))[0]
+        if last_part:
+            late = dict(enumerate(outs[:ways]))
+        else:
+            early = outs[:ways]
+            got.append({0: parts[0]} | held | send_all(parts, [m for m in everyone if m not in held]))
+    early = parts
+    late = lax.optimization_barrier((late, tuple(big_sums[:-1])))[0]
+    back = [{0: early[0]} | held, {0: late[0]}]
+    far = [m for m in everyone if m > 1 and m not in near]
+    for m in far + [1]:
+        back[0][m] = lax.ppermute(early[m], "block", [(i, i ^ m) for i in range(ways)])
+    evens_near = [m for m in near if m % 2 == 0]
+    odds_near = [m for m in near if m % 2]
+    for m in evens_near:
+        back[1][m] = lax.ppermute(late[m], "block", [(i, i ^ m) for i in range(ways)])
+    waits = [(m, back[0][far[i % len(far)]]) for i, m in enumerate(odds_near)]
+    waits += [(m, back[1][evens_near[i % len(evens_near)]]) for i, m in enumerate(far)]
+    for m, done in waits + [(1, back[0][1])]:
+        part, _ = lax.optimization_barrier((late[m], done))
+        back[1][m] = lax.ppermute(part, "block", [(i, i ^ m) for i in range(ways)])
+    returned = [[taken[m] for m in range(ways)] for taken in back]
+    back_specs = [
+        pl.BlockSpec((2, size, tile, rows), lambda i, me: (0, 0, i, 0))
+        for size in back_chunks
+        for _ in range(ways)
+    ]
+
+    small_share = 2 * MIDDLE * BLOCK_IN // n_dp // LANES
+    grad_tokens, small_grads = pl.pallas_call(
+        functools.partial(last_kernel, back_chunks, ways, n_dp, scale),
+        grid_spec=pltpu.PrefetchScalarGridSpec(
+            num_scalar_prefetch=1,
+            grid=(n_groups,),
+            in_specs=[token_spec, token_spec, right_spec, whole(perm_back)] + back_specs,
             out_specs=[
                 token_spec,
                 pl.BlockSpec((n_dp, GROUP, small_share, LANES), lambda i, me: (0, i, 0, 0)),
@@ -326,7 +408,7 @@
         compiler_params=params(),
         cost_estimate=cost(moved * BLOCK_IN * 6, 2 * moved),
         name="last",
-    )(me, tokens, cotangent, right_one, *in_hbm([part for parts in returned for part in parts]))
+    )(me, tokens, cotangent, right_one, perm_back, *in_hbm([part for parts in returned for part in parts]))
     small_grads, _ = lax.optimization_barrier((small_grads, big_sums[-1]))
     small_sum = summed(small_grads)
 
@@ -475,7 +557,7 @@
     )
     here = BLOCKS // mesh.shape["block"]
     ways = mesh.shape["block"]
-    fits = here % sum(CHUNKS) == 0 and here % GROUP == 0 and ways & (ways - 1) == 0
+    fits = here % sum(CHUNKS) == 0 and ways >= 8 and here % GROUP == 0 and ways & (ways - 1) == 0
     return jax.shard_map(
         on_device_fast if fits else on_device_plain, mesh=mesh, in_specs=in_specs, out_specs=out_specs, check_vma=False
     )

time: 339 us -> 309 us (0.912)
  waiting for transfers between devices: 192 us -> 166 us
  starting transfers between devices: 46.7 us -> 35 us
  Pallas kernels: 67.3 us -> 73.4 us
    ppermute x42 -> x35, waiting for transfers between devices: 171 us -> 145 us  [the longest x18 72.4 us: send(): taken = lax.ppermute(part, 'block', [(i, i ^ m) for i in range(ways)])]
    ppermute x42 -> x35, starting transfers between devices: 46.4 us -> 34.7 us  [the longest x18 16 us: send(): taken = lax.ppermute(part, 'block', [(i, i ^ m) for i in range(ways)])]
    pallas_call x4 -> x5, Pallas kernels: 44.6 us -> 50.7 us  [the longest x3 33.8 us: middle(): pl.pallas_call(functools.partial(middle_kernel, ways, len(old), n_dp, sca...]
  transfers between devices with their start and end apart: 46 -> 39, of which waited for: 22 -> 20; matrix products, arithmetic and copies ran while one was open for 5% -> 6% of each run, Pallas kernels for 16% -> 21%
where the time goes in v3:
time: 309 us
  waiting for transfers between devices  166 us (54%)
  Pallas kernels  73.4 us (24%)
  starting transfers between devices  35 us (11%)
  other arithmetic  17.7 us (6%)
  between operations  14 us (5%)
    ppermute x18, waiting for transfers between devices, send(): taken = lax.ppermute(part, 'block', [(i, i ^ m) for i in range(ways)])  72.4 us
    ppermute x5, waiting for transfers between devices, on_device_fast(): back[1][m] = lax.ppermute(part, 'block', [(i, i ^ m) for i in range(ways)])  34.7 us
    pallas_call x3, Pallas kernels, middle(): pl.pallas_call(functools.partial(middle_kernel, ways, len(old), n_dp, sca...  33.8 us
    ppermute x3, waiting for transfers between devices, on_device_fast(): lax.ppermute(early[m], 'block', [(i, i ^ m) for i in range(ways)])  23.6 us
    reduce_scatter x4, waiting for transfers between devices, summed(): return lax.psum_scatter(grads, 'dp', scatter_dimension=0, tiled=True)  21.2 us
    div x1, other arithmetic, on_device_fast(): adam_update = first_hat / (jnp.sqrt(second_hat) + 1e-08)  17.7 us
    ppermute x18, starting transfers between devices, send(): taken = lax.ppermute(part, 'block', [(i, i ^ m) for i in range(ways)])  16 us
    pallas_call x4, Pallas kernels, widen(): pl.pallas_call(functools.partial(widen_kernel, n_old), grid=(size // per_...  12.7 us
  transfers between devices with their start and end apart: 39, of which 20 were waited for; matrix products, arithmetic and copies ran while one was open for 6% of the time, Pallas kernels for 21%

profile of v3, /device:TPU:0, one launch (start us, length us, event | category | flops | bytes accessed | tf_op | source)
XLA Modules:
  0.0 308.9 jit_solution(12939091662453646004)
XLA Ops:
  7.2 6.2 %lead.1 = (bf16[2,2,48,512]{3,2,1,0:T(8,128)(2,1)}, bf16[2,2,48,512]{3,2,1,0:T(8,128)(2,1)}, bf16[2,2,48,512]{3,2,1,0:T(8,128)(2,1)}, bf16[2,2,48,512]{3,2,1,0:T...) custom-call(s32[1]{0:T(128)} %bitcast.me_ref, ...), custom_call_target="tpu_custom_call" | custom-call | flops 503316480 | bytes 4718592 | tf_op jit(solution)/shard_map/lead/pallas_call | solution.py:259
  21.5 3.3 %collective-permute-start.7 = (bf16[2,2,48,512]{3,2,1,0:T(8,128)(2,1)}, bf16[2,2,48,512]{3,2,1,0:T(8,128)(2,1)S(1)}, u32[]{:S(2)}, u32[]{:S(2)}) collective-permute-start(bf16[2,2,48,512]{3,2,1,0:T(8,128)(2,1)} %get-tuple-element.169), channel_id=1, source_target_pairs={{0,24},{4,28},{8,16},{12,20},{16,8},{20,12},{24,0},{28,4},{1,25},{... | collective-permute-start | bytes 589832 | tf_op jit(solution)/shard_map/ppermute | solution.py:329
  25.3 10.0 %first.1 = (bf16[2,4,48,512]{3,2,1,0:T(8,128)(2,1)}, bf16[2,4,48,512]{3,2,1,0:T(8,128)(2,1)}, bf16[2,4,48,512]{3,2,1,0:T(8,128)(2,1)}, bf16[2,4,48,512]{3,2,1,0:...) custom-call(s32[1]{0:T(128)} %bitcast.me_ref, ...), custom_call_target="tpu_custom_call" | custom-call | flops 3019898880 | bytes 9437184 | tf_op jit(solution)/shard_map/first/pallas_call | solution.py:331
  38.7 6.8 %middle.3 = (bf16[2,6,48,512]{3,2,1,0:T(8,128)(2,1)}, bf16[2,6,48,512]{3,2,1,0:T(8,128)(2,1)}, bf16[2,6,48,512]{3,2,1,0:T(8,128)(2,1)}, bf16[2,6,48,512]{3,2,1,0...) custom-call(s32[1]{0:T(128)} %bitcast.me_ref, ...), custom_call_target="tpu_custom_call" | custom-call | flops 2415919104 | bytes 6291456 | tf_op jit(solution)/shard_map/middle/pallas_call | solution.py:300
  51.4 10.0 %collective-permute-done.14.refs_6_ = bf16[2,4,48,512]{3,2,1,0:T(8,128)(2,1)S(1)} collective-permute-done((bf16[2,4,48,512]{3,2,1,0:T(8,128)(2,1)}, bf16[2,4,48,512]{3,2,1,0:T(8,128)(2,1)S(1)}, u32[]{:S(2)}, u32[]{:S(2)}) %collective-permute-start.14) | collective-permute-done | bytes 393248 | tf_op jit(solution)/shard_map/ppermute | solution.py:280
  61.4 8.3 %collective-permute-done.11.refs_5_ = bf16[2,4,48,512]{3,2,1,0:T(8,128)(2,1)S(1)} collective-permute-done((bf16[2,4,48,512]{3,2,1,0:T(8,128)(2,1)}, bf16[2,4,48,512]{3,2,1,0:T(8,128)(2,1)S(1)}, u32[]{:S(2)}, u32[]{:S(2)}) %collective-permute-start.11) | collective-permute-done | bytes 393248 | tf_op jit(solution)/shard_map/ppermute | solution.py:280
  72.6 3.8 %collective-permute-done.15.refs_7_ = bf16[2,4,48,512]{3,2,1,0:T(8,128)(2,1)} collective-permute-done((bf16[2,4,48,512]{3,2,1,0:T(8,128)(2,1)}, bf16[2,4,48,512]{3,2,1,0:T(8,128)(2,1)}, u32[]{:S(2)}, u32[]{:S(2)}) %collective-permute-start.15) | collective-permute-done | bytes 393248 | tf_op jit(solution)/shard_map/ppermute | solution.py:280
  76.4 11.3 %middle.4 = (bf16[2,6,48,512]{3,2,1,0:T(8,128)(2,1)}, bf16[2,6,48,512]{3,2,1,0:T(8,128)(2,1)}, bf16[2,6,48,512]{3,2,1,0:T(8,128)(2,1)}, bf16[2,6,48,512]{3,2,1,0...) custom-call(s32[1]{0:T(128)} %bitcast.me_ref, ...), custom_call_target="tpu_custom_call", output_to_operand_aliasing={{0}: (11, {}), {1}: (12, {}), {2}: (13, {}), {3}: (14, {}),... | custom-call | flops 4831838208 | bytes 12582912 | tf_op jit(solution)/shard_map/middle/pallas_call | solution.py:300
  92.8 12.0 %collective-permute-done.19.refs_5_ = bf16[2,6,48,512]{3,2,1,0:T(8,128)(2,1)S(1)} collective-permute-done((bf16[2,6,48,512]{3,2,1,0:T(8,128)(2,1)S(1)}, bf16[2,6,48,512]{3,2,1,0:T(8,128)(2,1)S(1)}, u32[]{:S(2)}, u32[]{:S(2)}) %collective-permute-start.19) | collective-permute-done | bytes 589856 | tf_op jit(solution)/shard_map/ppermute | solution.py:280
  107.6 12.0 %collective-permute-done.23.refs_6_ = bf16[2,6,48,512]{3,2,1,0:T(8,128)(2,1)S(1)} collective-permute-done((bf16[2,6,48,512]{3,2,1,0:T(8,128)(2,1)S(1)}, bf16[2,6,48,512]{3,2,1,0:T(8,128)(2,1)S(1)}, u32[]{:S(2)}, u32[]{:S(2)}) %collective-permute-start.23) | collective-permute-done | bytes 589856 | tf_op jit(solution)/shard_map/ppermute | solution.py:280
  119.7 12.5 %collective-permute-done.20.refs_4_ = bf16[2,6,48,512]{3,2,1,0:T(8,128)(2,1)S(1)} collective-permute-done((bf16[2,6,48,512]{3,2,1,0:T(8,128)(2,1)}, bf16[2,6,48,512]{3,2,1,0:T(8,128)(2,1)S(1)}, u32[]{:S(2)}, u32[]{:S(2)}) %collective-permute-start.20) | collective-permute-done | bytes 589856 | tf_op jit(solution)/shard_map/ppermute | solution.py:280
  135.0 9.6 %collective-permute-done.24.refs_7_ = bf16[2,6,48,512]{3,2,1,0:T(8,128)(2,1)} collective-permute-done((bf16[2,6,48,512]{3,2,1,0:T(8,128)(2,1)}, bf16[2,6,48,512]{3,2,1,0:T(8,128)(2,1)}, u32[]{:S(2)}, u32[]{:S(2)}) %collective-permute-start.24) | collective-permute-done | bytes 589856 | tf_op jit(solution)/shard_map/ppermute | solution.py:280
  144.6 15.7 %middle.5 = (bf16[2,6,48,512]{3,2,1,0:T(8,128)(2,1)}, bf16[2,6,48,512]{3,2,1,0:T(8,128)(2,1)}, bf16[2,6,48,512]{3,2,1,0:T(8,128)(2,1)}, bf16[2,6,48,512]{3,2,1,0...) custom-call(s32[1]{0:T(128)} %bitcast.me_ref, ...), custom_call_target="tpu_custom_call" | custom-call | flops 7247757312 | bytes 18874368 | tf_op jit(solution)/shard_map/middle/pallas_call | solution.py:300
  165.9 12.6 %collective-permute-done.26.refs_6_ = bf16[2,6,48,512]{3,2,1,0:T(8,128)(2,1)S(1)} collective-permute-done((bf16[2,6,48,512]{3,2,1,0:T(8,128)(2,1)}, bf16[2,6,48,512]{3,2,1,0:T(8,128)(2,1)S(1)}, u32[]{:S(2)}, u32[]{:S(2)}) %collective-permute-start.26) | collective-permute-done | bytes 589856 | tf_op jit(solution)/shard_map/ppermute | solution.py:374
  178.5 11.0 %collective-permute-done.27.refs_7_ = bf16[2,6,48,512]{3,2,1,0:T(8,128)(2,1)} collective-permute-done((bf16[2,6,48,512]{3,2,1,0:T(8,128)(2,1)}, bf16[2,6,48,512]{3,2,1,0:T(8,128)(2,1)}, u32[]{:S(2)}, u32[]{:S(2)}) %collective-permute-start.27) | collective-permute-done | bytes 589856 | tf_op jit(solution)/shard_map/ppermute | solution.py:374
  191.6 11.5 %collective-permute-done.29.refs_10_ = bf16[2,6,48,512]{3,2,1,0:T(8,128)(2,1)} collective-permute-done((bf16[2,6,48,512]{3,2,1,0:T(8,128)(2,1)}, bf16[2,6,48,512]{3,2,1,0:T(8,128)(2,1)}, u32[]{:S(2)}, u32[]{:S(2)}) %collective-permute-start.29) | collective-permute-done | bytes 589856 | tf_op jit(solution)/shard_map/ppermute | solution.py:378
  205.3 9.5 %collective-permute-done.30.refs_11_ = bf16[2,6,48,512]{3,2,1,0:T(8,128)(2,1)} collective-permute-done((bf16[2,6,48,512]{3,2,1,0:T(8,128)(2,1)}, bf16[2,6,48,512]{3,2,1,0:T(8,128)(2,1)}, u32[]{:S(2)}, u32[]{:S(2)}) %collective-permute-start.30) | collective-permute-done | bytes 589856 | tf_op jit(solution)/shard_map/ppermute | solution.py:383
  216.3 12.8 %collective-permute-done.33.refs_14_ = bf16[2,6,48,512]{3,2,1,0:T(8,128)(2,1)} collective-permute-done((bf16[2,6,48,512]{3,2,1,0:T(8,128)(2,1)}, bf16[2,6,48,512]{3,2,1,0:T(8,128)(2,1)}, u32[]{:S(2)}, u32[]{:S(2)}) %collective-permute-start.33) | collective-permute-done | bytes 589856 | tf_op jit(solution)/shard_map/ppermute | solution.py:383
  229.1 10.9 %collective-permute-done.34.refs_15_ = bf16[2,6,48,512]{3,2,1,0:T(8,128)(2,1)} collective-permute-done((bf16[2,6,48,512]{3,2,1,0:T(8,128)(2,1)}, bf16[2,6,48,512]{3,2,1,0:T(8,128)(2,1)}, u32[]{:S(2)}, u32[]{:S(2)}) %collective-permute-start.34) | collective-permute-done | bytes 589856 | tf_op jit(solution)/shard_map/ppermute | solution.py:383
  240.0 10.7 %last.1 = (bf16[512,1536]{1,0:T(8,128)(2,1)}, bf16[4,12,192,128]{3,2,1,0:T(8,128)(2,1)}) custom-call(s32[1]{0:T(128)} %bitcast.me_ref, bf16[512,1536]{1,0:T(8,128)(2,1)} %x_ref.5, bf16[512,1536]{1,0:T(8,128)(2,1)} %g_ref.5, bf16[12,128,384]{2,1,0:T(8,128)(2,1)} %right_ref.5, bf16[192,192]{1,0:T(8,128)(2,1)} %constant.33.clone.perm_ref, ...), custom_call_target="tpu_custom_call" | custom-call | flops 3623878656 | bytes 9437184 | tf_op jit(solution)/shard_map/last/pallas_call | solution.py:392
  250.7 17.7 %add_divide_fusion = (f32[12,122880]{1,0:T(8,128)}, f32[12,122880]{1,0:T(8,128)}, f32[12,122880]{1,0:T(8,128)}) fusion(f32[12,122880]{1,0:T(8,128)} %param.19, f32[12,122880]{1,0:T(8,128)} %param.21, f32[12,122880]{1,0:T(8,128)} %param.20), kind=kLoop, calls=%fused_computation.2 | loop fusion | flops 16220160 | bytes 35389440 | tf_op jit(solution)/shard_map/div | solution.py:235
  270.3 3.4 %widen.6 = (f32[12,128,384]{2,1,0:T(8,128)}, f32[12,96,512]{2,1,0:T(8,128)}) custom-call(bf16[1,4,768,128]{3,2,1,0:T(8,128)(2,1)} %reduce-scatter.7.cloned.1.call-done.sum_ref, f32[12,128,384]{2,1,0:T(8,128)} %get-tuple-element.289.refs_0_, f32[12,96,512]{2,1,0:T(8,128)} %get-tuple-element.290.refs_1_), custom_call_target="tpu_custom_call", output_to_operand_aliasing={{0}: (1, {}), {1}: (2, {})} | custom-call | bytes 2359296 | tf_op jit(solution)/shard_map/widen/pallas_call | solution.py:198
  273.7 4.6 %widen.7 = (f32[12,128,384]{2,1,0:T(8,128)}, f32[12,96,512]{2,1,0:T(8,128)}) custom-call(bf16[1,6,768,128]{3,2,1,0:T(8,128)(2,1)} %reduce-scatter.9.cloned.1.call-done.sum_ref, f32[12,128,384]{2,1,0:T(8,128)} %get-tuple-element.291.refs_0_, f32[12,96,512]{2,1,0:T(8,128)} %get-tuple-element.292.refs_1_), custom_call_target="tpu_custom_call", output_to_operand_aliasing={{0}: (1, {}), {1}: (2, {})} | custom-call | bytes 3538944 | tf_op jit(solution)/shard_map/widen/pallas_call | solution.py:198
  278.3 21.1 %reduce-scatter.11.cloned.1.call-done.sum_ref = bf16[1,12,192,128]{3,2,1,0:T(8,128)(2,1)} async-done(((bf16[4,12,192,128]{3,2,1,0:T(8,128)(2,1)}), bf16[1,12,192,128]{3,2,1,0:T(8,128)(2,1)}) %reduce-scatter.11.cloned.1.call-update) | async-done | bytes 589840 | tf_op jit(solution)/shard_map/reduce_scatter | solution.py:324
  (117 shorter events, 47.5 us)
Async XLA Ops:
  7.2 156.3 %reduce-scatter.5.cloned.1.call-start = ((), (), s32[]{:S(2)}) async-start(), calls=%async_computation.4 | async-start | bytes 1966080 | tf_op jit(solution)/shard_map/reduce_scatter | solution.py:324
  18.2 19.6 %collective-permute-start.6 = (bf16[2,2,48,512]{3,2,1,0:T(8,128)(2,1)}, bf16[2,2,48,512]{3,2,1,0:T(8,128)(2,1)S(1)}, u32[]{:S(2)}, u32[]{:S(2)}) collective-permute-start(bf16[2,2,48,512]{3,2,1,0:T(8,128)(2,1)} %get-tuple-element.168), channel_id=1, source_target_pairs={{0,16},{4,20},{8,24},{12,28},{16,0},{20,4},{24,8},{28,12},{1,17},{... | collective-permute-start | bytes 589832 | tf_op jit(solution)/shard_map/ppermute | solution.py:329
  48.1 115.4 %reduce-scatter.7.cloned.1.call-start = ((), (), s32[]{:S(2)}) async-start(), calls=%async_computation.5 | async-start | bytes 3932160 | tf_op jit(solution)/shard_map/reduce_scatter | solution.py:324
  49.6 20.1 %collective-permute-start.11 = (bf16[2,4,48,512]{3,2,1,0:T(8,128)(2,1)}, bf16[2,4,48,512]{3,2,1,0:T(8,128)(2,1)S(1)}, u32[]{:S(2)}, u32[]{:S(2)}) collective-permute-start(bf16[2,4,48,512]{3,2,1,0:T(8,128)(2,1)} %get-tuple-element.187), channel_id=1, source_target_pairs={{0,20},{4,16},{8,28},{12,24},{16,4},{20,0},{24,12},{28,8},{1,21},{... | collective-permute-start | bytes 1179656 | tf_op jit(solution)/shard_map/ppermute | solution.py:280
  50.0 19.7 %collective-permute-start.9 = (bf16[2,4,48,512]{3,2,1,0:T(8,128)(2,1)}, bf16[2,4,48,512]{3,2,1,0:T(8,128)(2,1)S(1)}, u32[]{:S(2)}, u32[]{:S(2)}) collective-permute-start(bf16[2,4,48,512]{3,2,1,0:T(8,128)(2,1)} %get-tuple-element.183), channel_id=1, source_target_pairs={{0,12},{4,8},{8,4},{12,0},{16,28},{20,24},{24,20},{28,16},{1,13},{... | collective-permute-start | bytes 1179656 | tf_op jit(solution)/shard_map/ppermute | solution.py:280
  51.4 20.5 %collective-permute-start.13 = (bf16[2,4,48,512]{3,2,1,0:T(8,128)(2,1)}, bf16[2,4,48,512]{3,2,1,0:T(8,128)(2,1)S(1)}, u32[]{:S(2)}, u32[]{:S(2)}) collective-permute-start(bf16[2,4,48,512]{3,2,1,0:T(8,128)(2,1)} %get-tuple-element.191), channel_id=1, source_target_pairs={{0,4},{4,0},{8,12},{12,8},{16,20},{20,16},{24,28},{28,24},{1,5},{5... | collective-permute-start | bytes 1179656 | tf_op jit(solution)/shard_map/ppermute | solution.py:280
  69.8 18.8 %collective-permute-start.10 = (bf16[2,6,48,512]{3,2,1,0:T(8,128)(2,1)}, bf16[2,6,48,512]{3,2,1,0:T(8,128)(2,1)}, u32[]{:S(2)}, u32[]{:S(2)}) collective-permute-start(bf16[2,6,48,512]{3,2,1,0:T(8,128)(2,1)} %get-tuple-element.184), channel_id=1, source_target_pairs={{0,8},{4,12},{8,0},{12,4},{16,24},{20,28},{24,16},{28,20},{1,9},{5... | collective-permute-start | bytes 1769480 | tf_op jit(solution)/shard_map/ppermute | solution.py:280
  89.5 161.2 %reduce-scatter.9.cloned.1.call-start = ((), (), s32[]{:S(2)}) async-start(), calls=%async_computation.6 | async-start | bytes 5898240 | tf_op jit(solution)/shard_map/reduce_scatter | solution.py:324
  91.5 28.1 %collective-permute-start.23 = (bf16[2,6,48,512]{3,2,1,0:T(8,128)(2,1)S(1)}, bf16[2,6,48,512]{3,2,1,0:T(8,128)(2,1)S(1)}, u32[]{:S(2)}, u32[]{:S(2)}) collective-permute-start(bf16[2,6,48,512]{3,2,1,0:T(8,128)(2,1)S(1)} %copy-done.12), channel_id=1, source_target_pairs={{0,24},{4,28},{8,16},{12,20},{16,8},{20,12},{24,0},{28,4},{1,25},{... | collective-permute-start | bytes 1769480 | tf_op jit(solution)/shard_map/ppermute | solution.py:280
  104.8 27.4 %collective-permute-start.20 = (bf16[2,6,48,512]{3,2,1,0:T(8,128)(2,1)}, bf16[2,6,48,512]{3,2,1,0:T(8,128)(2,1)S(1)}, u32[]{:S(2)}, u32[]{:S(2)}) collective-permute-start(bf16[2,6,48,512]{3,2,1,0:T(8,128)(2,1)} %get-tuple-element.235), channel_id=1, source_target_pairs={{0,16},{4,20},{8,24},{12,28},{16,0},{20,4},{24,8},{28,12},{1,17},{... | collective-permute-start | bytes 1769480 | tf_op jit(solution)/shard_map/ppermute | solution.py:280
  105.6 26.9 %collective-permute-start.17 = (bf16[2,6,48,512]{3,2,1,0:T(8,128)(2,1)}, bf16[2,6,48,512]{3,2,1,0:T(8,128)(2,1)S(1)}, u32[]{:S(2)}, u32[]{:S(2)}) collective-permute-start(bf16[2,6,48,512]{3,2,1,0:T(8,128)(2,1)} %get-tuple-element.231), channel_id=1, source_target_pairs={{0,8},{4,12},{8,0},{12,4},{16,24},{20,28},{24,16},{28,20},{1,9},{5... | collective-permute-start | bytes 1769480 | tf_op jit(solution)/shard_map/ppermute | solution.py:280
  107.3 26.9 %collective-permute-start.22 = (bf16[2,6,48,512]{3,2,1,0:T(8,128)(2,1)}, bf16[2,6,48,512]{3,2,1,0:T(8,128)(2,1)S(1)}, u32[]{:S(2)}, u32[]{:S(2)}) collective-permute-start(bf16[2,6,48,512]{3,2,1,0:T(8,128)(2,1)} %get-tuple-element.239), channel_id=1, source_target_pairs={{0,4},{4,0},{8,12},{12,8},{16,20},{20,16},{24,28},{28,24},{1,5},{5... | collective-permute-start | bytes 1769480 | tf_op jit(solution)/shard_map/ppermute | solution.py:280
  119.6 25.0 %collective-permute-start.24 = (bf16[2,6,48,512]{3,2,1,0:T(8,128)(2,1)}, bf16[2,6,48,512]{3,2,1,0:T(8,128)(2,1)}, u32[]{:S(2)}, u32[]{:S(2)}) collective-permute-start(bf16[2,6,48,512]{3,2,1,0:T(8,128)(2,1)} %get-tuple-element.243), channel_id=1, source_target_pairs={{0,28},{4,24},{8,20},{12,16},{16,12},{20,8},{24,4},{28,0},{1,29},{... | collective-permute-start | bytes 1769480 | tf_op jit(solution)/shard_map/ppermute | solution.py:280
  132.1 28.1 %collective-permute-start.21 = (bf16[2,6,48,512]{3,2,1,0:T(8,128)(2,1)}, bf16[2,6,48,512]{3,2,1,0:T(8,128)(2,1)S(1)}, u32[]{:S(2)}, u32[]{:S(2)}) collective-permute-start(bf16[2,6,48,512]{3,2,1,0:T(8,128)(2,1)} %get-tuple-element.236), channel_id=1, source_target_pairs={{0,20},{4,16},{8,28},{12,24},{16,4},{20,0},{24,12},{28,8},{1,21},{... | collective-permute-start | bytes 1769480 | tf_op jit(solution)/shard_map/ppermute | solution.py:280
  132.5 27.8 %collective-permute-start.18 = (bf16[2,6,48,512]{3,2,1,0:T(8,128)(2,1)}, bf16[2,6,48,512]{3,2,1,0:T(8,128)(2,1)}, u32[]{:S(2)}, u32[]{:S(2)}) collective-permute-start(bf16[2,6,48,512]{3,2,1,0:T(8,128)(2,1)} %get-tuple-element.232), channel_id=1, source_target_pairs={{0,12},{4,8},{8,4},{12,0},{16,28},{20,24},{24,20},{28,16},{1,13},{... | collective-permute-start | bytes 1769480 | tf_op jit(solution)/shard_map/ppermute | solution.py:280
  160.3 139.1 %reduce-scatter.11.cloned.1.call-start = ((), (), s32[]{:S(2)}) async-start(), calls=%async_computation.7 | async-start | bytes 2949120 | tf_op jit(solution)/shard_map/reduce_scatter | solution.py:324
  162.8 26.7 %collective-permute-start.27 = (bf16[2,6,48,512]{3,2,1,0:T(8,128)(2,1)}, bf16[2,6,48,512]{3,2,1,0:T(8,128)(2,1)}, u32[]{:S(2)}, u32[]{:S(2)}) collective-permute-start(bf16[2,6,48,512]{3,2,1,0:T(8,128)(2,1)} %get-tuple-element.260), channel_id=1, source_target_pairs={{0,28},{4,24},{8,20},{12,16},{16,12},{20,8},{24,4},{28,0},{1,29},{... | collective-permute-start | bytes 1769480 | tf_op jit(solution)/shard_map/ppermute | solution.py:374
  163.4 39.7 %collective-permute-start.29 = (bf16[2,6,48,512]{3,2,1,0:T(8,128)(2,1)}, bf16[2,6,48,512]{3,2,1,0:T(8,128)(2,1)}, u32[]{:S(2)}, u32[]{:S(2)}) collective-permute-start(bf16[2,6,48,512]{3,2,1,0:T(8,128)(2,1)} %get-tuple-element.274), channel_id=1, source_target_pairs={{0,8},{4,12},{8,0},{12,4},{16,24},{20,28},{24,16},{28,20},{1,9},{5... | collective-permute-start | bytes 1769480 | tf_op jit(solution)/shard_map/ppermute | solution.py:378
  164.9 40.4 %collective-permute-start.31 = (bf16[2,6,48,512]{3,2,1,0:T(8,128)(2,1)}, bf16[2,6,48,512]{3,2,1,0:T(8,128)(2,1)}, u32[]{:S(2)}, u32[]{:S(2)}) collective-permute-start(bf16[2,6,48,512]{3,2,1,0:T(8,128)(2,1)} %get-tuple-element.277), channel_id=1, source_target_pairs={{0,16},{4,20},{8,24},{12,28},{16,0},{20,4},{24,8},{28,12},{1,17},{... | collective-permute-start | bytes 1769480 | tf_op jit(solution)/shard_map/ppermute | solution.py:378
  165.7 39.6 %collective-permute-start.28 = (bf16[2,6,48,512]{3,2,1,0:T(8,128)(2,1)}, bf16[2,6,48,512]{3,2,1,0:T(8,128)(2,1)}, u32[]{:S(2)}, u32[]{:S(2)}) collective-permute-start(bf16[2,6,48,512]{3,2,1,0:T(8,128)(2,1)} %get-tuple-element.273), channel_id=1, source_target_pairs={{0,4},{4,0},{8,12},{12,8},{16,20},{20,16},{24,28},{28,24},{1,5},{5... | collective-permute-start | bytes 1769480 | tf_op jit(solution)/shard_map/ppermute | solution.py:383
  178.5 36.3 %collective-permute-start.30 = (bf16[2,6,48,512]{3,2,1,0:T(8,128)(2,1)}, bf16[2,6,48,512]{3,2,1,0:T(8,128)(2,1)}, u32[]{:S(2)}, u32[]{:S(2)}) collective-permute-start(bf16[2,6,48,512]{3,2,1,0:T(8,128)(2,1)} %get-tuple-element.276), channel_id=1, source_target_pairs={{0,12},{4,8},{8,4},{12,0},{16,28},{20,24},{24,20},{28,16},{1,13},{... | collective-permute-start | bytes 1769480 | tf_op jit(solution)/shard_map/ppermute | solution.py:383
  189.5 26.7 %collective-permute-start.32 = (bf16[2,6,48,512]{3,2,1,0:T(8,128)(2,1)}, bf16[2,6,48,512]{3,2,1,0:T(8,128)(2,1)}, u32[]{:S(2)}, u32[]{:S(2)}) collective-permute-start(bf16[2,6,48,512]{3,2,1,0:T(8,128)(2,1)} %get-tuple-element.279), channel_id=1, source_target_pairs={{0,20},{4,16},{8,28},{12,24},{16,4},{20,0},{24,12},{28,8},{1,21},{... | collective-permute-start | bytes 1769480 | tf_op jit(solution)/shard_map/ppermute | solution.py:383
  203.1 26.0 %collective-permute-start.33 = (bf16[2,6,48,512]{3,2,1,0:T(8,128)(2,1)}, bf16[2,6,48,512]{3,2,1,0:T(8,128)(2,1)}, u32[]{:S(2)}, u32[]{:S(2)}) collective-permute-start(bf16[2,6,48,512]{3,2,1,0:T(8,128)(2,1)} %get-tuple-element.281), channel_id=1, source_target_pairs={{0,24},{4,28},{8,16},{12,20},{16,8},{20,12},{24,0},{28,4},{1,25},{... | collective-permute-start | bytes 1769480 | tf_op jit(solution)/shard_map/ppermute | solution.py:383
  205.3 34.7 %collective-permute-start.34 = (bf16[2,6,48,512]{3,2,1,0:T(8,128)(2,1)}, bf16[2,6,48,512]{3,2,1,0:T(8,128)(2,1)}, u32[]{:S(2)}, u32[]{:S(2)}) collective-permute-start(bf16[2,6,48,512]{3,2,1,0:T(8,128)(2,1)} %get-tuple-element.283), channel_id=1, source_target_pairs={{0,28},{4,24},{8,20},{12,16},{16,12},{20,8},{24,4},{28,0},{1,29},{... | collective-permute-start | bytes 1769480 | tf_op jit(solution)/shard_map/ppermute | solution.py:383
  (39 other events, 681.9 us)
Sparse Core Ops, SparseCore 0:
  48.2 35.5 reduce-scatter.4
  89.6 60.6 reduce-scatter.6
  160.4 85.6 reduce-scatter.8
  250.8 48.5 reduce-scatter.10

commit v4 on v3

--- a/solution.py
+++ b/solution.py
@@ -19,7 +19,7 @@
 BF16 = jnp.bfloat16
 GROUP = 4
 LANES = 128
-VMEM_LIMIT = 62 * 1024 * 1024
+VMEM_LIMIT = 65000 * 1024
 CHUNKS = (2, 4, 6)
 
 
@@ -38,7 +38,7 @@
     return one_hot(rows.transpose(1, 0, 2).reshape(-1), rows.size)
 
 
-def first_kernel(chunks, ways, me_ref, x_ref, g_ref, right_ref, left_ref, perm_ref, *refs):
+def first_kernel(chunks, skip, ways, me_ref, x_ref, g_ref, right_ref, left_ref, perm_ref, *refs):
     outs, (rows,) = refs[:-1], refs[-1:]
     here = sum(chunks)
     span = here * SPLIT
@@ -57,8 +57,8 @@
                 [rows[which, b, pl.ds(start, span), :] for b in range(GROUP)], axis=0
             )
             mixed = dot(perm, taken, 1, 0).astype(BF16)
-            at = chunks[0]
-            for k, size in enumerate(chunks[1:]):
+            at = sum(chunks[:skip])
+            for k, size in enumerate(chunks[skip:]):
                 part = mixed[at * GROUP * SPLIT : (at + size) * GROUP * SPLIT]
                 outs[k * ways + m][which] = part.reshape(size, GROUP * SPLIT, part.shape[-1])
                 at += size
@@ -246,30 +246,34 @@
         pltpu.HBM((2, size, span, rows), BF16) for size in chunks for _ in range(ways)
     ]
     moved = 2 * here * MIDDLE * rows
+    offsets = [sum(chunks[:k]) for k in range(len(chunks))]
+    n_parts = len(chunks)
     first_in_specs = [token_spec, token_spec, right_spec, left_spec]
-    lead_perm = permutation(ways * chunks[0], GROUP)
-    lead_rows = np.arange(MIDDLE).reshape(ways, here, SPLIT)[:, : chunks[0]]
-    lead_pick = one_hot(lead_rows.reshape(-1), MIDDLE)
 
     def whole(array):
         return pl.BlockSpec(array.shape, lambda i, me: (0, 0))
 
     perm = permutation(here, GROUP)
     perm_back = permutation(GROUP, here)
-    lead = pl.pallas_call(
-        functools.partial(lead_kernel, chunks[0], ways),
-        grid_spec=pltpu.PrefetchScalarGridSpec(
-            num_scalar_prefetch=1,
-            grid=(n_groups,),
-            in_specs=first_in_specs + [whole(lead_perm), whole(lead_pick)],
-            out_specs=part_specs[:ways],
-            scratch_shapes=[pltpu.VMEM((ways * chunks[0] * tile, rows), BF16)],
-        ),
-        out_shape=part_shapes[:ways],
-        compiler_params=params(),
-        cost_estimate=cost(moved * BLOCK_IN * chunks[0] / here * 5, moved),
-        name="lead",
-    )(me, tokens, cotangent, right_one, left_two, lead_perm, lead_pick)
+    def lead(k):
+        size, at = chunks[k], offsets[k]
+        mix = permutation(ways * size, GROUP)
+        pick = np.arange(MIDDLE).reshape(ways, here, SPLIT)[:, at : at + size]
+        pick = one_hot(pick.reshape(-1), MIDDLE)
+        return pl.pallas_call(
+            functools.partial(lead_kernel, size, ways),
+            grid_spec=pltpu.PrefetchScalarGridSpec(
+                num_scalar_prefetch=1,
+                grid=(n_groups,),
+                in_specs=first_in_specs + [whole(mix), whole(pick)],
+                out_specs=part_specs[k * ways : (k + 1) * ways],
+                scratch_shapes=[pltpu.VMEM((ways * size * tile, rows), BF16)],
+            ),
+            out_shape=part_shapes[k * ways : (k + 1) * ways],
+            compiler_params=params(),
+            cost_estimate=cost(moved * BLOCK_IN * size / here * 5, moved),
+            name="lead",
+        )(me, tokens, cotangent, right_one, left_two, mix, pick)
 
     lane_done = {}
 
@@ -288,8 +292,6 @@
     odds = list(range(1, ways, 2))
     near = [m for m in range(2, ways) if (m // 2) & (m // 2 - 1) == 0]
     everyone = evens + odds
-    offsets = [sum(chunks[:k]) for k in range(len(chunks))]
-    n_parts = len(chunks)
 
     share = (BLOCK_HID * MIDDLE + MIDDLE * BLOCK_HID) // n_dp // LANES
     def middle(k, takes, old, first_give, n_give):
@@ -323,36 +325,40 @@
     def summed(grads):
         return lax.psum_scatter(grads, "dp", scatter_dimension=0, tiled=True)
 
-    queue = [dict(enumerate(lead))]
-    got = [{0: lead[0]}]
+    queue = [dict(enumerate(lead(0)))]
+    got = [{0: queue[0][0]}]
     for m in near + [m for m in everyone if m not in near]:
-        got[0][m] = lax.ppermute(lead[m], "block", [(i, i ^ m) for i in range(ways)])
+        got[0][m] = lax.ppermute(queue[0][m], "block", [(i, i ^ m) for i in range(ways)])
         lane_done[m // 2] = got[0][m]
+    queue += [dict(enumerate(lead(k))) for k in range(1, n_parts - 1)]
     rest = pl.pallas_call(
-        functools.partial(first_kernel, chunks, ways),
+        functools.partial(first_kernel, chunks, n_parts - 1, ways),
         grid_spec=pltpu.PrefetchScalarGridSpec(
             num_scalar_prefetch=1,
             grid=(n_groups,),
             in_specs=first_in_specs + [whole(perm)],
-            out_specs=part_specs[ways:],
+            out_specs=part_specs[-ways:],
             scratch_shapes=[pltpu.VMEM((2, GROUP, MIDDLE, rows), BF16)],
         ),
-        out_shape=part_shapes[ways:],
+        out_shape=part_shapes[-ways:],
         compiler_params=params(),
         cost_estimate=cost(moved * BLOCK_IN * 5, 2 * moved),
         name="first",
     )(me, tokens, cotangent, right_one, left_two, perm)
-    for k in range(n_parts - 1):
-        queue.append(dict(enumerate(rest[k * ways : (k + 1) * ways])))
+    queue.append(dict(enumerate(rest)))
 
     early_size = offsets[-1]
     back_chunks = (early_size, chunks[-1])
     big_sums, early, held = [], (), {}
+    far = [m for m in everyone if m > 1 and m not in near]
     for k in range(n_parts):
         last_part = k + 1 == n_parts
         if last_part:
             parts = dict(enumerate(early))
-            ahead = send_all(parts, [m for m in near if m % 2 == 0] + [m for m in near if m % 2])
+            ahead = send_all(parts, [m for m in near if m % 2 == 0])
+            for m, before in zip([m for m in near if m % 2], far):
+                lane_done[m // 2] = got[k][before]
+                ahead[m] = send(parts, m)
             outs = middle(k, [got[k][m] for m in range(ways)], (), 0, chunks[-1])
         else:
             parts = queue[k + 1]
@@ -365,11 +371,15 @@
             late = dict(enumerate(outs[:ways]))
         else:
             early = outs[:ways]
+            if k + 2 == n_parts:
+                for m in far:
+                    lane_done.pop(m // 2, None)
+                    held[m] = send(parts, m)
+                    lane_done.pop(m // 2, None)
             got.append({0: parts[0]} | held | send_all(parts, [m for m in everyone if m not in held]))
     early = parts
     late = lax.optimization_barrier((late, tuple(big_sums[:-1])))[0]
     back = [{0: early[0]} | held, {0: late[0]}]
-    far = [m for m in everyone if m > 1 and m not in near]
     for m in far + [1]:
         back[0][m] = lax.ppermute(early[m], "block", [(i, i ^ m) for i in range(ways)])
     evens_near = [m for m in near if m % 2 == 0]
@@ -418,7 +428,7 @@
         big = widen(big_sums[k], big_shapes, here, offsets[k], big, 1)
     grad_right_two, grad_left_one = big
     small_shapes = ((MIDDLE // n_dp, BLOCK_IN), (BLOCK_IN // n_dp, MIDDLE))
-    grad_left_two, grad_right_one = widen(small_sum, small_shapes, here, 0, (), GROUP)
+    grad_left_two, grad_right_one = widen(small_sum, small_shapes, here, 0, (), here)
     return (
         grad_tokens,
         grad_right_one,

time: 309 us -> 303 us (0.981)
  waiting for transfers between devices: 166 us -> 156 us
  Pallas kernels: 73.4 us -> 79.5 us
    ppermute x18, waiting for transfers between devices: 72.4 us -> 60 us  [send(): taken = lax.ppermute(part, 'block', [(i, i ^ m) for i in range(ways)])]
    pallas_call x2 -> x3, Pallas kernels: 16.2 us -> 23.1 us  [the longest x2 13.5 us: lead(): pl.pallas_call(functools.partial(lead_kernel, size, ways), grid_spec=pltp...]
  transfers between devices with their start and end apart: 39 -> 39, of which waited for: 20 -> 22; matrix products, arithmetic and copies ran while one was open for 6% -> 6% of each run, Pallas kernels for 21% -> 24%
where the time goes in v4:
time: 303 us
  waiting for transfers between devices  156 us (51%)
  Pallas kernels  79.5 us (26%)
  starting transfers between devices  35.9 us (12%)
  other arithmetic  17.8 us (6%)
  between operations  13.9 us (5%)
    ppermute x18, waiting for transfers between devices, send(): taken = lax.ppermute(part, 'block', [(i, i ^ m) for i in range(ways)])  60 us
    ppermute x5, waiting for transfers between devices, on_device_fast(): back[1][m] = lax.ppermute(part, 'block', [(i, i ^ m) for i in range(ways)])  35 us
    pallas_call x3, Pallas kernels, middle(): pl.pallas_call(functools.partial(middle_kernel, ways, len(old), n_dp, sca...  33.8 us
    ppermute x3, waiting for transfers between devices, on_device_fast(): lax.ppermute(early[m], 'block', [(i, i ^ m) for i in range(ways)])  23.8 us
    reduce_scatter x4, waiting for transfers between devices, summed(): return lax.psum_scatter(grads, 'dp', scatter_dimension=0, tiled=True)  21.2 us
    div x1, other arithmetic, on_device_fast(): adam_update = first_hat / (jnp.sqrt(second_hat) + 1e-08)  17.8 us
    ppermute x18, starting transfers between devices, send(): taken = lax.ppermute(part, 'block', [(i, i ^ m) for i in range(ways)])  17.1 us
    pallas_call x2, Pallas kernels, lead(): pl.pallas_call(functools.partial(lead_kernel, size, ways), grid_spec=pltp...  13.5 us
  transfers between devices with their start and end apart: 39, of which 22 were waited for; matrix products, arithmetic and copies ran while one was open for 6% of the time, Pallas kernels for 24%

profile of v4, /device:TPU:0, one launch (start us, length us, event | category | flops | bytes accessed | tf_op | source)
XLA Modules:
  0.0 302.6 jit_solution(15261785379731482675)
XLA Ops:
  7.2 6.2 %lead.3 = (bf16[2,2,48,512]{3,2,1,0:T(8,128)(2,1)}, bf16[2,2,48,512]{3,2,1,0:T(8,128)(2,1)}, bf16[2,2,48,512]{3,2,1,0:T(8,128)(2,1)}, bf16[2,2,48,512]{3,2,1,0:T...) custom-call(s32[1]{0:T(128)} %bitcast.me_ref, ...), custom_call_target="tpu_custom_call" | custom-call | flops 503316480 | bytes 4718592 | tf_op jit(solution)/shard_map/lead/pallas_call | solution.py:263
  21.5 3.3 %collective-permute-start.7 = (bf16[2,2,48,512]{3,2,1,0:T(8,128)(2,1)}, bf16[2,2,48,512]{3,2,1,0:T(8,128)(2,1)}, u32[]{:S(2)}, u32[]{:S(2)}) collective-permute-start(bf16[2,2,48,512]{3,2,1,0:T(8,128)(2,1)} %get-tuple-element.167), channel_id=1, source_target_pairs={{0,24},{4,28},{8,16},{12,20},{16,8},{20,12},{24,0},{28,4},{1,25},{... | collective-permute-start | bytes 589832 | tf_op jit(solution)/shard_map/ppermute | solution.py:331
  25.4 7.3 %lead.2 = (bf16[2,4,48,512]{3,2,1,0:T(8,128)(2,1)}, bf16[2,4,48,512]{3,2,1,0:T(8,128)(2,1)}, bf16[2,4,48,512]{3,2,1,0:T(8,128)(2,1)}, bf16[2,4,48,512]{3,2,1,0:T...) custom-call(s32[1]{0:T(128)} %bitcast.me_ref, ...), custom_call_target="tpu_custom_call" | custom-call | flops 1006632960 | bytes 4718592 | tf_op jit(solution)/shard_map/lead/pallas_call | solution.py:263
  36.1 6.8 %middle.3 = (bf16[2,6,48,512]{3,2,1,0:T(8,128)(2,1)}, bf16[2,6,48,512]{3,2,1,0:T(8,128)(2,1)}, bf16[2,6,48,512]{3,2,1,0:T(8,128)(2,1)}, bf16[2,6,48,512]{3,2,1,0...) custom-call(s32[1]{0:T(128)} %bitcast.me_ref, ...), custom_call_target="tpu_custom_call" | custom-call | flops 2415919104 | bytes 6291456 | tf_op jit(solution)/shard_map/middle/pallas_call | solution.py:302
  48.7 10.0 %collective-permute-done.14.refs_6_ = bf16[2,4,48,512]{3,2,1,0:T(8,128)(2,1)S(1)} collective-permute-done((bf16[2,4,48,512]{3,2,1,0:T(8,128)(2,1)}, bf16[2,4,48,512]{3,2,1,0:T(8,128)(2,1)S(1)}, u32[]{:S(2)}, u32[]{:S(2)}) %collective-permute-start.14) | collective-permute-done | bytes 393248 | tf_op jit(solution)/shard_map/ppermute | solution.py:284
  58.7 9.5 %first.1 = (bf16[2,6,48,512]{3,2,1,0:T(8,128)(2,1)}, bf16[2,6,48,512]{3,2,1,0:T(8,128)(2,1)}, bf16[2,6,48,512]{3,2,1,0:T(8,128)(2,1)}, bf16[2,6,48,512]{3,2,1,0:...) custom-call(s32[1]{0:T(128)} %bitcast.me_ref, ...), custom_call_target="tpu_custom_call" | custom-call | flops 3019898880 | bytes 9437184 | tf_op jit(solution)/shard_map/first/pallas_call | solution.py:334
  70.3 3.4 %collective-permute-done.15.refs_7_ = bf16[2,4,48,512]{3,2,1,0:T(8,128)(2,1)} collective-permute-done((bf16[2,4,48,512]{3,2,1,0:T(8,128)(2,1)}, bf16[2,4,48,512]{3,2,1,0:T(8,128)(2,1)}, u32[]{:S(2)}, u32[]{:S(2)}) %collective-permute-start.15) | collective-permute-done | bytes 393248 | tf_op jit(solution)/shard_map/ppermute | solution.py:284
  73.7 11.3 %middle.4 = (bf16[2,6,48,512]{3,2,1,0:T(8,128)(2,1)}, bf16[2,6,48,512]{3,2,1,0:T(8,128)(2,1)}, bf16[2,6,48,512]{3,2,1,0:T(8,128)(2,1)}, bf16[2,6,48,512]{3,2,1,0...) custom-call(s32[1]{0:T(128)} %bitcast.me_ref, ...), custom_call_target="tpu_custom_call", output_to_operand_aliasing={{0}: (11, {}), {1}: (12, {}), {2}: (13, {}), {3}: (14, {}),... | custom-call | flops 4831838208 | bytes 12582912 | tf_op jit(solution)/shard_map/middle/pallas_call | solution.py:302
  91.8 10.8 %collective-permute-done.20.refs_5_ = bf16[2,6,48,512]{3,2,1,0:T(8,128)(2,1)} collective-permute-done((bf16[2,6,48,512]{3,2,1,0:T(8,128)(2,1)}, bf16[2,6,48,512]{3,2,1,0:T(8,128)(2,1)}, u32[]{:S(2)}, u32[]{:S(2)}) %collective-permute-start.20) | collective-permute-done | bytes 589856 | tf_op jit(solution)/shard_map/ppermute | solution.py:284
  104.7 12.6 %collective-permute-done.18.refs_6_ = bf16[2,6,48,512]{3,2,1,0:T(8,128)(2,1)} collective-permute-done((bf16[2,6,48,512]{3,2,1,0:T(8,128)(2,1)}, bf16[2,6,48,512]{3,2,1,0:T(8,128)(2,1)}, u32[]{:S(2)}, u32[]{:S(2)}) %collective-permute-start.18) | collective-permute-done | bytes 589856 | tf_op jit(solution)/shard_map/ppermute | solution.py:284
  117.8 10.9 %collective-permute-done.22.refs_7_ = bf16[2,6,48,512]{3,2,1,0:T(8,128)(2,1)} collective-permute-done((bf16[2,6,48,512]{3,2,1,0:T(8,128)(2,1)}, bf16[2,6,48,512]{3,2,1,0:T(8,128)(2,1)}, u32[]{:S(2)}, u32[]{:S(2)}) %collective-permute-start.22) | collective-permute-done | bytes 589856 | tf_op jit(solution)/shard_map/ppermute | solution.py:284
  130.5 15.7 %middle.5 = (bf16[2,6,48,512]{3,2,1,0:T(8,128)(2,1)}, bf16[2,6,48,512]{3,2,1,0:T(8,128)(2,1)}, bf16[2,6,48,512]{3,2,1,0:T(8,128)(2,1)}, bf16[2,6,48,512]{3,2,1,0...) custom-call(s32[1]{0:T(128)} %bitcast.me_ref, ...), custom_call_target="tpu_custom_call" | custom-call | flops 7247757312 | bytes 18874368 | tf_op jit(solution)/shard_map/middle/pallas_call | solution.py:302
  146.2 7.3 %collective-permute-done.19.refs_3_ = bf16[2,6,48,512]{3,2,1,0:T(8,128)(2,1)} collective-permute-done((bf16[2,6,48,512]{3,2,1,0:T(8,128)(2,1)}, bf16[2,6,48,512]{3,2,1,0:T(8,128)(2,1)}, u32[]{:S(2)}, u32[]{:S(2)}) %collective-permute-start.19) | collective-permute-done | bytes 589856 | tf_op jit(solution)/shard_map/ppermute | solution.py:284
  159.7 12.6 %collective-permute-done.26.refs_6_ = bf16[2,6,48,512]{3,2,1,0:T(8,128)(2,1)} collective-permute-done((bf16[2,6,48,512]{3,2,1,0:T(8,128)(2,1)}, bf16[2,6,48,512]{3,2,1,0:T(8,128)(2,1)}, u32[]{:S(2)}, u32[]{:S(2)}) %collective-permute-start.26) | collective-permute-done | bytes 589856 | tf_op jit(solution)/shard_map/ppermute | solution.py:384
  172.8 11.1 %collective-permute-done.27.refs_7_ = bf16[2,6,48,512]{3,2,1,0:T(8,128)(2,1)} collective-permute-done((bf16[2,6,48,512]{3,2,1,0:T(8,128)(2,1)}, bf16[2,6,48,512]{3,2,1,0:T(8,128)(2,1)}, u32[]{:S(2)}, u32[]{:S(2)}) %collective-permute-start.27) | collective-permute-done | bytes 589856 | tf_op jit(solution)/shard_map/ppermute | solution.py:384
  185.3 11.8 %collective-permute-done.29.refs_10_ = bf16[2,6,48,512]{3,2,1,0:T(8,128)(2,1)} collective-permute-done((bf16[2,6,48,512]{3,2,1,0:T(8,128)(2,1)}, bf16[2,6,48,512]{3,2,1,0:T(8,128)(2,1)}, u32[]{:S(2)}, u32[]{:S(2)}) %collective-permute-start.29) | collective-permute-done | bytes 589856 | tf_op jit(solution)/shard_map/ppermute | solution.py:388
  199.4 9.2 %collective-permute-done.30.refs_11_ = bf16[2,6,48,512]{3,2,1,0:T(8,128)(2,1)} collective-permute-done((bf16[2,6,48,512]{3,2,1,0:T(8,128)(2,1)}, bf16[2,6,48,512]{3,2,1,0:T(8,128)(2,1)}, u32[]{:S(2)}, u32[]{:S(2)}) %collective-permute-start.30) | collective-permute-done | bytes 589856 | tf_op jit(solution)/shard_map/ppermute | solution.py:393
  210.0 12.9 %collective-permute-done.33.refs_14_ = bf16[2,6,48,512]{3,2,1,0:T(8,128)(2,1)} collective-permute-done((bf16[2,6,48,512]{3,2,1,0:T(8,128)(2,1)}, bf16[2,6,48,512]{3,2,1,0:T(8,128)(2,1)}, u32[]{:S(2)}, u32[]{:S(2)}) %collective-permute-start.33) | collective-permute-done | bytes 589856 | tf_op jit(solution)/shard_map/ppermute | solution.py:393
  222.9 11.5 %collective-permute-done.34.refs_15_ = bf16[2,6,48,512]{3,2,1,0:T(8,128)(2,1)} collective-permute-done((bf16[2,6,48,512]{3,2,1,0:T(8,128)(2,1)}, bf16[2,6,48,512]{3,2,1,0:T(8,128)(2,1)}, u32[]{:S(2)}, u32[]{:S(2)}) %collective-permute-start.34) | collective-permute-done | bytes 589856 | tf_op jit(solution)/shard_map/ppermute | solution.py:393
  234.4 10.6 %last.1 = (bf16[512,1536]{1,0:T(8,128)(2,1)}, bf16[4,12,192,128]{3,2,1,0:T(8,128)(2,1)}) custom-call(s32[1]{0:T(128)} %bitcast.me_ref, bf16[512,1536]{1,0:T(8,128)(2,1)} %x_ref.7, bf16[512,1536]{1,0:T(8,128)(2,1)} %g_ref.7, bf16[12,128,384]{2,1,0:T(8,128)(2,1)} %right_ref.7, bf16[192,192]{1,0:T(8,128)(2,1)} %constant.35.clone.perm_ref, ...), custom_call_target="tpu_custom_call" | custom-call | flops 3623878656 | bytes 9437184 | tf_op jit(solution)/shard_map/last/pallas_call | solution.py:402
  245.1 17.8 %add_divide_fusion = (f32[12,122880]{1,0:T(8,128)}, f32[12,122880]{1,0:T(8,128)}, f32[12,122880]{1,0:T(8,128)}) fusion(f32[12,122880]{1,0:T(8,128)} %param.21, f32[12,122880]{1,0:T(8,128)} %param.23, f32[12,122880]{1,0:T(8,128)} %param.22), kind=kLoop, calls=%fused_computation.2 | loop fusion | flops 16220160 | bytes 35389440 | tf_op jit(solution)/shard_map/div | solution.py:235
  264.7 3.4 %widen.6 = (f32[12,128,384]{2,1,0:T(8,128)}, f32[12,96,512]{2,1,0:T(8,128)}) custom-call(bf16[1,4,768,128]{3,2,1,0:T(8,128)(2,1)} %reduce-scatter.7.cloned.1.call-done.sum_ref, f32[12,128,384]{2,1,0:T(8,128)} %get-tuple-element.285.refs_0_, f32[12,96,512]{2,1,0:T(8,128)} %get-tuple-element.286.refs_1_), custom_call_target="tpu_custom_call", output_to_operand_aliasing={{0}: (1, {}), {1}: (2, {})} | custom-call | bytes 2359296 | tf_op jit(solution)/shard_map/widen/pallas_call | solution.py:198
  268.1 4.6 %widen.7 = (f32[12,128,384]{2,1,0:T(8,128)}, f32[12,96,512]{2,1,0:T(8,128)}) custom-call(bf16[1,6,768,128]{3,2,1,0:T(8,128)(2,1)} %reduce-scatter.9.cloned.1.call-done.sum_ref, f32[12,128,384]{2,1,0:T(8,128)} %get-tuple-element.287.refs_0_, f32[12,96,512]{2,1,0:T(8,128)} %get-tuple-element.288.refs_1_), custom_call_target="tpu_custom_call", output_to_operand_aliasing={{0}: (1, {}), {1}: (2, {})} | custom-call | bytes 3538944 | tf_op jit(solution)/shard_map/widen/pallas_call | solution.py:198
  272.7 21.2 %reduce-scatter.11.cloned.1.call-done.sum_ref = bf16[1,12,192,128]{3,2,1,0:T(8,128)(2,1)} async-done(((bf16[4,12,192,128]{3,2,1,0:T(8,128)(2,1)}), bf16[1,12,192,128]{3,2,1,0:T(8,128)(2,1)}) %reduce-scatter.11.cloned.1.call-update) | async-done | bytes 589840 | tf_op jit(solution)/shard_map/reduce_scatter | solution.py:326
  (76 shorter events, 46.9 us)
Async XLA Ops:
  7.2 150.4 %reduce-scatter.5.cloned.1.call-start = ((), (), s32[]{:S(2)}) async-start(), calls=%async_computation.4 | async-start | bytes 1966080 | tf_op jit(solution)/shard_map/reduce_scatter | solution.py:326
  45.4 112.2 %reduce-scatter.7.cloned.1.call-start = ((), (), s32[]{:S(2)}) async-start(), calls=%async_computation.5 | async-start | bytes 3932160 | tf_op jit(solution)/shard_map/reduce_scatter | solution.py:326
  46.9 21.3 %collective-permute-start.11 = (bf16[2,4,48,512]{3,2,1,0:T(8,128)(2,1)}, bf16[2,4,48,512]{3,2,1,0:T(8,128)(2,1)}, u32[]{:S(2)}, u32[]{:S(2)}) collective-permute-start(bf16[2,4,48,512]{3,2,1,0:T(8,128)(2,1)} %get-tuple-element.185), channel_id=1, source_target_pairs={{0,20},{4,16},{8,28},{12,24},{16,4},{20,0},{24,12},{28,8},{1,21},{... | collective-permute-start | bytes 1179656 | tf_op jit(solution)/shard_map/ppermute | solution.py:284
  47.3 20.9 %collective-permute-start.9 = (bf16[2,4,48,512]{3,2,1,0:T(8,128)(2,1)}, bf16[2,4,48,512]{3,2,1,0:T(8,128)(2,1)}, u32[]{:S(2)}, u32[]{:S(2)}) collective-permute-start(bf16[2,4,48,512]{3,2,1,0:T(8,128)(2,1)} %get-tuple-element.181), channel_id=1, source_target_pairs={{0,12},{4,8},{8,4},{12,0},{16,28},{20,24},{24,20},{28,16},{1,13},{... | collective-permute-start | bytes 1179656 | tf_op jit(solution)/shard_map/ppermute | solution.py:284
  48.7 21.6 %collective-permute-start.13 = (bf16[2,4,48,512]{3,2,1,0:T(8,128)(2,1)}, bf16[2,4,48,512]{3,2,1,0:T(8,128)(2,1)}, u32[]{:S(2)}, u32[]{:S(2)}) collective-permute-start(bf16[2,4,48,512]{3,2,1,0:T(8,128)(2,1)} %get-tuple-element.189), channel_id=1, source_target_pairs={{0,4},{4,0},{8,12},{12,8},{16,20},{20,16},{24,28},{28,24},{1,5},{5... | collective-permute-start | bytes 1179656 | tf_op jit(solution)/shard_map/ppermute | solution.py:284
  68.2 18.0 %collective-permute-start.10 = (bf16[2,6,48,512]{3,2,1,0:T(8,128)(2,1)}, bf16[2,6,48,512]{3,2,1,0:T(8,128)(2,1)}, u32[]{:S(2)}, u32[]{:S(2)}) collective-permute-start(bf16[2,6,48,512]{3,2,1,0:T(8,128)(2,1)} %get-tuple-element.182), channel_id=1, source_target_pairs={{0,8},{4,12},{8,0},{12,4},{16,24},{20,28},{24,16},{28,20},{1,9},{5... | collective-permute-start | bytes 1769480 | tf_op jit(solution)/shard_map/ppermute | solution.py:284
  86.8 158.3 %reduce-scatter.9.cloned.1.call-start = ((), (), s32[]{:S(2)}) async-start(), calls=%async_computation.6 | async-start | bytes 5898240 | tf_op jit(solution)/shard_map/reduce_scatter | solution.py:326
  88.8 28.5 %collective-permute-start.18 = (bf16[2,6,48,512]{3,2,1,0:T(8,128)(2,1)}, bf16[2,6,48,512]{3,2,1,0:T(8,128)(2,1)}, u32[]{:S(2)}, u32[]{:S(2)}) collective-permute-start(bf16[2,6,48,512]{3,2,1,0:T(8,128)(2,1)} %get-tuple-element.230), channel_id=1, source_target_pairs={{0,24},{4,28},{8,16},{12,20},{16,8},{20,12},{24,0},{28,4},{1,25},{... | collective-permute-start | bytes 1769480 | tf_op jit(solution)/shard_map/ppermute | solution.py:284
  90.1 38.6 %collective-permute-start.22 = (bf16[2,6,48,512]{3,2,1,0:T(8,128)(2,1)}, bf16[2,6,48,512]{3,2,1,0:T(8,128)(2,1)}, u32[]{:S(2)}, u32[]{:S(2)}) collective-permute-start(bf16[2,6,48,512]{3,2,1,0:T(8,128)(2,1)} %get-tuple-element.235), channel_id=1, source_target_pairs={{0,28},{4,24},{8,20},{12,16},{16,12},{20,8},{24,4},{28,0},{1,29},{... | collective-permute-start | bytes 1769480 | tf_op jit(solution)/shard_map/ppermute | solution.py:284
  91.1 39.4 %collective-permute-start.24 = (bf16[2,6,48,512]{3,2,1,0:T(8,128)(2,1)}, bf16[2,6,48,512]{3,2,1,0:T(8,128)(2,1)}, u32[]{:S(2)}, u32[]{:S(2)}) collective-permute-start(bf16[2,6,48,512]{3,2,1,0:T(8,128)(2,1)} %get-tuple-element.239), channel_id=1, source_target_pairs={{0,4},{4,0},{8,12},{12,8},{16,20},{20,16},{24,28},{28,24},{1,5},{5... | collective-permute-start | bytes 1769480 | tf_op jit(solution)/shard_map/ppermute | solution.py:284
  102.6 43.6 %collective-permute-start.21 = (bf16[2,6,48,512]{3,2,1,0:T(8,128)(2,1)}, bf16[2,6,48,512]{3,2,1,0:T(8,128)(2,1)}, u32[]{:S(2)}, u32[]{:S(2)}) collective-permute-start(bf16[2,6,48,512]{3,2,1,0:T(8,128)(2,1)} %get-tuple-element.234), channel_id=1, source_target_pairs={{0,16},{4,20},{8,24},{12,28},{16,0},{20,4},{24,8},{28,12},{1,17},{... | collective-permute-start | bytes 1769480 | tf_op jit(solution)/shard_map/ppermute | solution.py:284
  103.4 42.8 %collective-permute-start.17 = (bf16[2,6,48,512]{3,2,1,0:T(8,128)(2,1)}, bf16[2,6,48,512]{3,2,1,0:T(8,128)(2,1)}, u32[]{:S(2)}, u32[]{:S(2)}) collective-permute-start(bf16[2,6,48,512]{3,2,1,0:T(8,128)(2,1)} %get-tuple-element.229), channel_id=1, source_target_pairs={{0,8},{4,12},{8,0},{12,4},{16,24},{20,28},{24,16},{28,20},{1,9},{5... | collective-permute-start | bytes 1769480 | tf_op jit(solution)/shard_map/ppermute | solution.py:284
  117.3 36.2 %collective-permute-start.19 = (bf16[2,6,48,512]{3,2,1,0:T(8,128)(2,1)}, bf16[2,6,48,512]{3,2,1,0:T(8,128)(2,1)}, u32[]{:S(2)}, u32[]{:S(2)}) collective-permute-start(bf16[2,6,48,512]{3,2,1,0:T(8,128)(2,1)} %get-tuple-element.231), channel_id=1, source_target_pairs={{0,12},{4,8},{8,4},{12,0},{16,28},{20,24},{24,20},{28,16},{1,13},{... | collective-permute-start | bytes 1769480 | tf_op jit(solution)/shard_map/ppermute | solution.py:284
  128.7 25.7 %collective-permute-start.23 = (bf16[2,6,48,512]{3,2,1,0:T(8,128)(2,1)}, bf16[2,6,48,512]{3,2,1,0:T(8,128)(2,1)}, u32[]{:S(2)}, u32[]{:S(2)}) collective-permute-start(bf16[2,6,48,512]{3,2,1,0:T(8,128)(2,1)} %get-tuple-element.236), channel_id=1, source_target_pairs={{0,20},{4,16},{8,28},{12,24},{16,4},{20,0},{24,12},{28,8},{1,21},{... | collective-permute-start | bytes 1769480 | tf_op jit(solution)/shard_map/ppermute | solution.py:284
  154.5 139.5 %reduce-scatter.11.cloned.1.call-start = ((), (), s32[]{:S(2)}) async-start(), calls=%async_computation.7 | async-start | bytes 2949120 | tf_op jit(solution)/shard_map/reduce_scatter | solution.py:326
  154.9 17.5 %collective-permute-start.26 = (bf16[2,6,48,512]{3,2,1,0:T(8,128)(2,1)}, bf16[2,6,48,512]{3,2,1,0:T(8,128)(2,1)}, u32[]{:S(2)}, u32[]{:S(2)}) collective-permute-start(bf16[2,6,48,512]{3,2,1,0:T(8,128)(2,1)} %get-tuple-element.255), channel_id=1, source_target_pairs={{0,24},{4,28},{8,16},{12,20},{16,8},{20,12},{24,0},{28,4},{1,25},{... | collective-permute-start | bytes 1769480 | tf_op jit(solution)/shard_map/ppermute | solution.py:384
  156.6 27.3 %collective-permute-start.27 = (bf16[2,6,48,512]{3,2,1,0:T(8,128)(2,1)}, bf16[2,6,48,512]{3,2,1,0:T(8,128)(2,1)}, u32[]{:S(2)}, u32[]{:S(2)}) collective-permute-start(bf16[2,6,48,512]{3,2,1,0:T(8,128)(2,1)} %get-tuple-element.256), channel_id=1, source_target_pairs={{0,28},{4,24},{8,20},{12,16},{16,12},{20,8},{24,4},{28,0},{1,29},{... | collective-permute-start | bytes 1769480 | tf_op jit(solution)/shard_map/ppermute | solution.py:384
  157.5 39.5 %collective-permute-start.29 = (bf16[2,6,48,512]{3,2,1,0:T(8,128)(2,1)}, bf16[2,6,48,512]{3,2,1,0:T(8,128)(2,1)}, u32[]{:S(2)}, u32[]{:S(2)}) collective-permute-start(bf16[2,6,48,512]{3,2,1,0:T(8,128)(2,1)} %get-tuple-element.270), channel_id=1, source_target_pairs={{0,8},{4,12},{8,0},{12,4},{16,24},{20,28},{24,16},{28,20},{1,9},{5... | collective-permute-start | bytes 1769480 | tf_op jit(solution)/shard_map/ppermute | solution.py:388
  159.4 40.1 %collective-permute-start.31 = (bf16[2,6,48,512]{3,2,1,0:T(8,128)(2,1)}, bf16[2,6,48,512]{3,2,1,0:T(8,128)(2,1)}, u32[]{:S(2)}, u32[]{:S(2)}) collective-permute-start(bf16[2,6,48,512]{3,2,1,0:T(8,128)(2,1)} %get-tuple-element.273), channel_id=1, source_target_pairs={{0,16},{4,20},{8,24},{12,28},{16,0},{20,4},{24,8},{28,12},{1,17},{... | collective-permute-start | bytes 1769480 | tf_op jit(solution)/shard_map/ppermute | solution.py:388
  159.7 39.7 %collective-permute-start.28 = (bf16[2,6,48,512]{3,2,1,0:T(8,128)(2,1)}, bf16[2,6,48,512]{3,2,1,0:T(8,128)(2,1)}, u32[]{:S(2)}, u32[]{:S(2)}) collective-permute-start(bf16[2,6,48,512]{3,2,1,0:T(8,128)(2,1)} %get-tuple-element.269), channel_id=1, source_target_pairs={{0,4},{4,0},{8,12},{12,8},{16,20},{20,16},{24,28},{28,24},{1,5},{5... | collective-permute-start | bytes 1769480 | tf_op jit(solution)/shard_map/ppermute | solution.py:393
  172.4 36.2 %collective-permute-start.30 = (bf16[2,6,48,512]{3,2,1,0:T(8,128)(2,1)}, bf16[2,6,48,512]{3,2,1,0:T(8,128)(2,1)}, u32[]{:S(2)}, u32[]{:S(2)}) collective-permute-start(bf16[2,6,48,512]{3,2,1,0:T(8,128)(2,1)} %get-tuple-element.272), channel_id=1, source_target_pairs={{0,12},{4,8},{8,4},{12,0},{16,28},{20,24},{24,20},{28,16},{1,13},{... | collective-permute-start | bytes 1769480 | tf_op jit(solution)/shard_map/ppermute | solution.py:393
  183.9 26.1 %collective-permute-start.32 = (bf16[2,6,48,512]{3,2,1,0:T(8,128)(2,1)}, bf16[2,6,48,512]{3,2,1,0:T(8,128)(2,1)}, u32[]{:S(2)}, u32[]{:S(2)}) collective-permute-start(bf16[2,6,48,512]{3,2,1,0:T(8,128)(2,1)} %get-tuple-element.275), channel_id=1, source_target_pairs={{0,20},{4,16},{8,28},{12,24},{16,4},{20,0},{24,12},{28,8},{1,21},{... | collective-permute-start | bytes 1769480 | tf_op jit(solution)/shard_map/ppermute | solution.py:393
  197.1 25.8 %collective-permute-start.33 = (bf16[2,6,48,512]{3,2,1,0:T(8,128)(2,1)}, bf16[2,6,48,512]{3,2,1,0:T(8,128)(2,1)}, u32[]{:S(2)}, u32[]{:S(2)}) collective-permute-start(bf16[2,6,48,512]{3,2,1,0:T(8,128)(2,1)} %get-tuple-element.277), channel_id=1, source_target_pairs={{0,24},{4,28},{8,16},{12,20},{16,8},{20,12},{24,0},{28,4},{1,25},{... | collective-permute-start | bytes 1769480 | tf_op jit(solution)/shard_map/ppermute | solution.py:393
  199.4 35.0 %collective-permute-start.34 = (bf16[2,6,48,512]{3,2,1,0:T(8,128)(2,1)}, bf16[2,6,48,512]{3,2,1,0:T(8,128)(2,1)}, u32[]{:S(2)}, u32[]{:S(2)}) collective-permute-start(bf16[2,6,48,512]{3,2,1,0:T(8,128)(2,1)} %get-tuple-element.279), channel_id=1, source_target_pairs={{0,28},{4,24},{8,20},{12,16},{16,12},{20,8},{24,4},{28,0},{1,29},{... | collective-permute-start | bytes 1769480 | tf_op jit(solution)/shard_map/ppermute | solution.py:393
  (18 other events, 236.8 us)
Sparse Core Ops, SparseCore 0:
  45.5 35.6 reduce-scatter.4
  86.9 60.6 reduce-scatter.6
  154.6 85.9 reduce-scatter.8
  245.2 48.6 reduce-scatter.10
